TPU v7x, 32 devices: a whole 2x2x4 slice. The times are simulated.
32 devices in a mesh: row: 4 (over y, core), col: 8 (over z, x).
Axes of the slice: x: 2, y: 2, z: 4, core: 2. Of those that a mesh axis runs over, the one named last changes fastest.
Arguments:
- tokens: bfloat16 [256, 16384], P('row', 'col'), may hold values from -6 to 6
- out_grad: bfloat16 [256, 16384], P('row', 'col'), may hold values from -6 to 6
- gate_values: bfloat16 [4, 8, 56, 128, 128], P('row', 'col'), may hold values from -0.3125 to 0.3125
- gate_exps: int32 [4, 8, 56], P('row', 'col'), may hold values from -1 to 1
- up_values: bfloat16 [4, 8, 56, 128, 128], P('row', 'col'), may hold values from -0.3125 to 0.3125
- up_exps: int32 [4, 8, 56], P('row', 'col'), may hold values from -1 to 1
- gate_up_ids: int32 [4, 8, 56], P('row', 'col'), may hold values from 0 to 896, as said below
- down_values: bfloat16 [4, 8, 56, 128, 128], P('row', 'col'), may hold values from -0.25 to 0.25
- down_exps: int32 [4, 8, 56], P('row', 'col'), may hold values from -1 to 1
- down_ids: int32 [4, 8, 56], P('row', 'col'), may hold values from 0 to 896, as said below
Outputs:
- output: bfloat16 [256, 16384], P('row', 'col')
- input_grad: bfloat16 [256, 16384], P('row', 'col')
- gate_grad: bfloat16 [4, 8, 56, 128, 128], P('row', 'col')
- up_grad: bfloat16 [4, 8, 56, 128, 128], P('row', 'col')
- down_grad: bfloat16 [4, 8, 56, 128, 128], P('row', 'col')
Inputs may be any that keep to these rules, and one draw needn't show every extreme that they name: `gate_up_ids`: for each device (first two indices) the live entries name distinct blocks below 896 and come first; the value 896 marks an empty slot; on some device all 56 slots are live. `down_ids`: as for gate_up_ids.
All inputs are finite; a program needn't handle non-finite values.
Results may differ from a plain program's by a relative error of at most 0.005.
Values may be sent and summed in bfloat16 or wider, within the bound.
A program may use at most 320 MiB of HBM per device.

v0:
```python
import jax
import jax.numpy as jnp
from jax import lax
from jax.sharding import PartitionSpec as P

FF_WIN = 28672


def exponent_scale(exponents):
    return jnp.where(exponents < 0, 0.5, jnp.where(exponents > 0, 2.0, 1.0)).astype(jnp.float32)


def scaled_slots(values, exponents):
    scales = exponent_scale(exponents[0, 0])
    return (values[0, 0].astype(jnp.float32) * scales[:, None, None]).astype(jnp.bfloat16)


def slot_indices(block_ids, out_blocks, in_blocks):
    block_count = out_blocks * in_blocks
    live_slot = block_ids < block_count
    out_index = jnp.where(live_slot, block_ids // in_blocks, out_blocks)
    in_index = jnp.where(live_slot, block_ids % in_blocks, in_blocks)
    return (live_slot, out_index, in_index)


def dense_matrix(scaled, block_ids, out_blocks, in_blocks):
    block_size = scaled.shape[-1]
    block_count = out_blocks * in_blocks
    placed = (
        jnp.zeros((block_count + 1, block_size, block_size), jnp.bfloat16)
        .at[block_ids]
        .set(scaled)[:block_count]
    )
    shaped = placed.reshape(out_blocks, in_blocks, block_size, block_size).transpose(0, 2, 1, 3)
    return shaped.reshape(out_blocks * block_size, in_blocks * block_size)


def project(activations, scaled, block_ids, out_blocks, in_blocks, transposed):
    matrix = dense_matrix(scaled, block_ids, out_blocks, in_blocks)
    if transposed:
        return jnp.dot(activations, matrix, preferred_element_type=jnp.float32)
    return lax.dot_general(
        activations, matrix, (((1,), (1,)), ((), ())), preferred_element_type=jnp.float32
    )


def block_grad(out_acts, in_acts, exponents, block_ids, out_blocks, in_blocks):
    block_size = out_acts.shape[1] // out_blocks
    scales = exponent_scale(exponents)
    live_slot, out_index, in_index = slot_indices(block_ids, out_blocks, in_blocks)
    dense = lax.dot_general(
        out_acts, in_acts, (((0,), (0,)), ((), ())), preferred_element_type=jnp.float32
    )
    shaped = dense.reshape(out_blocks, block_size, in_blocks, block_size).transpose(0, 2, 1, 3)
    shaped = shaped.reshape(out_blocks * in_blocks, block_size, block_size)
    grads = jnp.take(shaped, block_ids, axis=0, mode="clip")
    kept = jnp.where(live_slot[:, None, None], grads * scales[:, None, None], 0.0)
    return kept.astype(jnp.bfloat16)[None, None]


def activate(gate_sum, up_sum):
    return (jax.nn.silu(gate_sum) * up_sum).astype(jnp.bfloat16)


def derive(hidden_grad, gate_sum, up_sum):
    sigmoid_gate = jax.nn.sigmoid(gate_sum)
    gate_piece = (
        hidden_grad * up_sum * sigmoid_gate * (1.0 + gate_sum * (1.0 - sigmoid_gate))
    ).astype(jnp.bfloat16)
    up_piece = (hidden_grad * jax.nn.silu(gate_sum)).astype(jnp.bfloat16)
    return (gate_piece, up_piece)


def on_device(
    tokens,
    out_grad,
    gate_values,
    gate_exps,
    up_values,
    up_exps,
    gate_up_ids,
    down_values,
    down_exps,
    down_ids,
):
    block_size = gate_values.shape[-1]
    tokens_all, grads_all = (
        lax.all_gather(tokens, "row", axis=0, tiled=True),
        lax.all_gather(out_grad, "row", axis=0, tiled=True),
    )
    width_blocks = tokens_all.shape[1] // block_size
    hidden_blocks = FF_WIN // lax.axis_size("row") // block_size
    gate_scaled = scaled_slots(gate_values, gate_exps)
    up_scaled = scaled_slots(up_values, up_exps)
    down_scaled = scaled_slots(down_values, down_exps)
    pair_slots = gate_up_ids[0, 0]
    down_slots = down_ids[0, 0]
    gate_part = project(tokens_all, gate_scaled, pair_slots, hidden_blocks, width_blocks, False)
    up_part = project(tokens_all, up_scaled, pair_slots, hidden_blocks, width_blocks, False)
    gate_share, up_share = (
        lax.psum_scatter(gate_part, "col", scatter_dimension=0, tiled=True),
        lax.psum_scatter(up_part, "col", scatter_dimension=0, tiled=True),
    )
    hidden = lax.all_gather(activate(gate_share, up_share), "col", axis=0, tiled=True)
    output_part = project(hidden, down_scaled, down_slots, width_blocks, hidden_blocks, False)
    back_part = project(grads_all, down_scaled, down_slots, width_blocks, hidden_blocks, True)
    grad_share = lax.psum_scatter(back_part, "col", scatter_dimension=0, tiled=True)
    gate_piece, up_piece = derive(grad_share, gate_share, up_share)
    gate_act_grad, up_act_grad = (
        lax.all_gather(gate_piece, "col", axis=0, tiled=True),
        lax.all_gather(up_piece, "col", axis=0, tiled=True),
    )
    input_part = project(gate_act_grad, gate_scaled, pair_slots, hidden_blocks, width_blocks, True)
    input_part = input_part + project(
        up_act_grad, up_scaled, pair_slots, hidden_blocks, width_blocks, True
    )
    output_rows, input_rows = (
        lax.psum_scatter(output_part, "row", scatter_dimension=0, tiled=True),
        lax.psum_scatter(input_part, "row", scatter_dimension=0, tiled=True),
    )
    gate_grad = block_grad(
        gate_act_grad, tokens_all, gate_exps[0, 0], pair_slots, hidden_blocks, width_blocks
    )
    up_grad = block_grad(
        up_act_grad, tokens_all, up_exps[0, 0], pair_slots, hidden_blocks, width_blocks
    )
    down_grad = block_grad(
        grads_all, hidden, down_exps[0, 0], down_slots, width_blocks, hidden_blocks
    )
    return (
        output_rows.astype(jnp.bfloat16),
        input_rows.astype(jnp.bfloat16),
        gate_grad,
        up_grad,
        down_grad,
    )


def solution(mesh):
    in_specs = (
        P("row", "col"),
        P("row", "col"),
        P("row", "col", None, None, None),
        P("row", "col", None),
        P("row", "col", None, None, None),
        P("row", "col", None),
        P("row", "col", None),
        P("row", "col", None, None, None),
        P("row", "col", None),
        P("row", "col", None),
    )
    out_specs = (
        P("row", "col"),
        P("row", "col"),
        P("row", "col", None, None, None),
        P("row", "col", None, None, None),
        P("row", "col", None, None, None),
    )
    return jax.shard_map(
        on_device, mesh=mesh, in_specs=in_specs, out_specs=out_specs, check_vma=False
    )
```

profile of v0, /device:TPU:0, one launch (start us, length us, event | category | flops | bytes accessed | tf_op | source)
XLA Modules:
  0.0 1102.7 jit_solution(9671710017425499287)
XLA Ops:
  31.4 20.2 %slice.23 = bf16[896,128,128]{2,1,0:T(8,128)(2,1)} slice(bf16[897,128,128]{2,1,0:T(8,128)(2,1)} %scatter_fusion.2), slice={[0:896], [0:128], [0:128]} | slice | bytes 58720256 | tf_op jit(solution)/shard_map/slice | solution.py:30
  51.6 32.4 %copy.38 = bf16[16,128,56,128]{3,2,1,0:T(8,128)(2,1)} copy(bf16[16,128,56,128]{3,1,2,0:T(8,128)(2,1)} %bitcast.136) | data formatting | bytes 58720256 | tf_op jit(solution)/shard_map/transpose | solution.py:34
  84.0 20.3 %fusion.24 = f32[256,7168]{0,1:T(8,128)} fusion(bf16[256,2048]{1,0:T(8,128)(2,1)} %all-gather.10.cloned.1.call-done, bf16[256,8,56,128]{3,2,1,0:T(8,128)(2,1)} %bitcast.142), kind=kOutput, calls=%fused_computation.29 | convolution fusion | flops 7516192768 | bytes 37748736 | tf_op jit(solution)/shard_map/dot_general | solution.py:41
  135.0 20.6 %slice.21 = bf16[896,128,128]{2,1,0:T(8,128)(2,1)} slice(bf16[897,128,128]{2,1,0:T(8,128)(2,1)} %scatter_fusion), slice={[0:896], [0:128], [0:128]} | slice | bytes 58720256 | tf_op jit(solution)/shard_map/slice | solution.py:30
  155.6 27.1 %copy.33 = bf16[56,128,16,128]{3,2,1,0:T(8,128)(2,1)} copy(bf16[56,128,16,128]{3,1,2,0:T(8,128)(2,1)} %bitcast.137) | data formatting | bytes 58720256 | tf_op jit(solution)/shard_map/transpose | solution.py:34
  182.6 19.3 %fusion.18 = f32[256,7168]{0,1:T(8,128)} fusion(bf16[256,2048]{1,0:T(8,128)(2,1)} %all-gather.6.cloned.1.call-done, bf16[896,8,16,128]{3,2,1,0:T(8,128)(2,1)} %bitcast.144), kind=kOutput, calls=%fused_computation.27 | convolution fusion | flops 7516192768 | bytes 37748736 | tf_op jit(solution)/shard_map/dot_general | solution.py:42
  232.0 20.4 %slice.22 = bf16[896,128,128]{2,1,0:T(8,128)(2,1)} slice(bf16[897,128,128]{2,1,0:T(8,128)(2,1)} %scatter_fusion.1), slice={[0:896], [0:128], [0:128]} | slice | bytes 58720256 | tf_op jit(solution)/shard_map/slice | solution.py:30
  252.4 27.0 %copy.36 = bf16[56,128,16,128]{3,2,1,0:T(8,128)(2,1)} copy(bf16[56,128,16,128]{3,1,2,0:T(8,128)(2,1)} %bitcast.138) | data formatting | bytes 58720256 | tf_op jit(solution)/shard_map/transpose | solution.py:34
  279.4 18.9 %fusion.21 = f32[256,7168]{0,1:T(8,128)} fusion(bf16[256,2048]{1,0:T(8,128)(2,1)S(1)} %copy-done.1, bf16[896,8,16,128]{3,2,1,0:T(8,128)(2,1)} %bitcast.146), kind=kOutput, calls=%fused_computation.28 | convolution fusion | flops 7516192768 | bytes 37748736 | tf_op jit(solution)/shard_map/dot_general | solution.py:42
  306.8 76.4 %reduce-scatter.16.cloned.1.call-done = f32[32,7168]{1,0:T(8,128)} async-done(((f32[256,7168]{1,0:T(8,128)}), f32[32,7168]{1,0:T(8,128)}) %reduce-scatter.16.cloned.1.call-update) | async-done | bytes 917520 | tf_op jit(solution)/shard_map/reduce_scatter | solution.py:101
  383.2 135.3 %reduce-scatter.18.cloned.1.call-done = f32[32,7168]{1,0:T(8,128)} async-done(((f32[256,7168]{1,0:T(8,128)}), f32[32,7168]{1,0:T(8,128)}) %reduce-scatter.18.cloned.1.call-update) | async-done | bytes 917520 | tf_op jit(solution)/shard_map/reduce_scatter | solution.py:102
  523.5 64.3 %all-gather.14.cloned.1.call-done = bf16[256,7168]{1,0:T(8,128)(2,1)} async-done(((bf16[32,7168]{1,0:T(8,128)(2,1)}), bf16[256,7168]{1,0:T(8,128)(2,1)}) %all-gather.14.cloned.1.call-update) | async-done | bytes 3670032 | tf_op jit(solution)/shard_map/all_gather | solution.py:111
  602.6 53.2 %all-gather.12.cloned.1.call-done = bf16[256,7168]{1,0:T(8,128)(2,1)} async-done(((bf16[32,7168]{1,0:T(8,128)(2,1)}), bf16[256,7168]{1,0:T(8,128)(2,1)}) %all-gather.12.cloned.1.call-update) | async-done | bytes 3670032 | tf_op jit(solution)/shard_map/all_gather | solution.py:110
  672.0 51.9 %all-gather.8.cloned.1.call-done = bf16[256,7168]{1,0:T(8,128)(2,1)} async-done(((bf16[32,7168]{1,0:T(8,128)(2,1)}), bf16[256,7168]{1,0:T(8,128)(2,1)}) %all-gather.8.cloned.1.call-update) | async-done | bytes 3670032 | tf_op jit(solution)/shard_map/all_gather | solution.py:104
  723.9 16.1 %fusion.2 = f32[256,2048]{1,0:T(8,128)} fusion(bf16[256,7168]{1,0:T(8,128)(2,1)} %all-gather.8.cloned.1.call-done, bf16[256,8,56,128]{3,2,1,0:T(8,128)(2,1)} %bitcast.143), kind=kOutput, calls=%fused_computation.8 | convolution fusion | flops 7516192768 | bytes 35127296 | tf_op jit(solution)/shard_map/dot_general | solution.py:42
  742.3 22.9 %convolution_bitcast_fusion = f32[896,8,16,128]{3,1,2,0:T(8,128)} fusion(bf16[256,7168]{1,0:T(8,128)(2,1)} %all-gather.8.cloned.1.call-done, bf16[256,2048]{1,0:T(8,128)(2,1)S(1)} %copy-done.3), kind=kOutput, calls=%fused_computation.24 | convolution fusion | flops 7516192768 | bytes 63438848 | tf_op jit(solution)/shard_map/dot_general | solution.py:51
  765.1 40.5 %copy.57 = f32[896,8,16,128]{3,2,1,0:T(8,128)} copy(f32[896,8,16,128]{3,1,2,0:T(8,128)} %convolution_bitcast_fusion) | data formatting | bytes 117440512
  805.6 53.7 %copy.45 = f32[16,128,56,128]{3,1,2,0:T(8,128)} copy(f32[16,128,56,128]{1,0,3,2:T(8,128)} %bitcast.133) | data formatting | bytes 117440512 | tf_op jit(solution)/shard_map/reshape | solution.py:54
  859.3 22.5 %convolution_bitcast_fusion.2 = f32[896,8,16,128]{3,1,2,0:T(8,128)} fusion(bf16[256,7168]{1,0:T(8,128)(2,1)} %all-gather.12.cloned.1.call-done, bf16[256,2048]{1,0:T(8,128)(2,1)S(1)} %copy-done.2), kind=kOutput, calls=%fused_computation.26 | convolution fusion | flops 7516192768 | bytes 63438848 | tf_op jit(solution)/shard_map/dot_general | solution.py:51
  881.8 39.8 %copy.55 = f32[896,8,16,128]{3,2,1,0:T(8,128)} copy(f32[896,8,16,128]{3,1,2,0:T(8,128)} %convolution_bitcast_fusion.2) | data formatting | bytes 117440512
  921.6 40.6 %copy.43 = f32[56,128,16,128]{3,1,2,0:T(8,128)} copy(f32[56,128,16,128]{3,2,1,0:T(8,128)} %bitcast.134) | data formatting | bytes 117440512 | tf_op jit(solution)/shard_map/reshape | solution.py:54
  962.2 22.6 %convolution_bitcast_fusion.1 = f32[896,8,16,128]{3,1,2,0:T(8,128)} fusion(bf16[256,7168]{1,0:T(8,128)(2,1)} %all-gather.14.cloned.1.call-done, bf16[256,2048]{1,0:T(8,128)(2,1)S(1)} %copy-done.2), kind=kOutput, calls=%fused_computation.25 | convolution fusion | flops 7516192768 | bytes 63438848 | tf_op jit(solution)/shard_map/dot_general | solution.py:51
  984.8 39.5 %copy.56 = f32[896,8,16,128]{3,2,1,0:T(8,128)} copy(f32[896,8,16,128]{3,1,2,0:T(8,128)} %convolution_bitcast_fusion.1) | data formatting | bytes 117440512
  1024.4 40.4 %copy.44 = f32[56,128,16,128]{3,1,2,0:T(8,128)} copy(f32[56,128,16,128]{3,2,1,0:T(8,128)} %bitcast.135) | data formatting | bytes 117440512 | tf_op jit(solution)/shard_map/reshape | solution.py:54
  (89 shorter events, 162.2 us)
Async XLA Ops:
  7.2 76.8 %all-gather.10.cloned.1.call-start = ((), (), s32[]{:S(2)}) async-start(), calls=%async_computation.8 | async-start | bytes 1310720 | tf_op jit(solution)/shard_map/all_gather | solution.py:89
  7.9 174.7 %all-gather.6.cloned.1.call-start = ((), (), s32[]{:S(2)}) async-start(), calls=%async_computation.5 | async-start | bytes 1310720 | tf_op jit(solution)/shard_map/all_gather | solution.py:88
  8.6 298.2 %reduce-scatter.20.cloned.1.call-start = ((), (), s32[]{:S(2)}) async-start(), calls=%async_computation.14 | async-start | bytes 8257536 | tf_op jit(solution)/shard_map/reduce_scatter | solution.py:107
  112.6 0.7 copy-start.15
  112.6 0.7 copy-start.16
  112.7 270.6 %reduce-scatter.16.cloned.1.call-start = ((), (), s32[]{:S(2)}) async-start(), calls=%async_computation.12 | async-start | bytes 8257536 | tf_op jit(solution)/shard_map/reduce_scatter | solution.py:101
  113.3 97.5 %copy-start.6 = (f32[56]{0:T(128)}, f32[56]{0:T(128)S(1)}, u32[]{:S(2)}) copy-start(f32[56]{0:T(128)S(1)} %get-tuple-element.11) | copy-start | bytes 676
  210.4 308.1 %reduce-scatter.18.cloned.1.call-start = ((), (), s32[]{:S(2)}) async-start(), calls=%async_computation.13 | async-start | bytes 8257536 | tf_op jit(solution)/shard_map/reduce_scatter | solution.py:102
  252.4 27.0 %copy-start.1 = (bf16[256,2048]{1,0:T(8,128)(2,1)S(1)}, bf16[256,2048]{1,0:T(8,128)(2,1)}, u32[]{:S(2)}) copy-start(bf16[256,2048]{1,0:T(8,128)(2,1)} %all-gather.6.cloned.1.call-done) | copy-start | bytes 3145732
  306.7 281.1 %all-gather.14.cloned.1.call-start = ((), (), s32[]{:S(2)}) async-start(), calls=%async_computation.10 | async-start | bytes 4128768 | tf_op jit(solution)/shard_map/all_gather | solution.py:111
  521.7 134.1 %all-gather.12.cloned.1.call-start = ((), (), s32[]{:S(2)}) async-start(), calls=%async_computation.9 | async-start | bytes 4128768 | tf_op jit(solution)/shard_map/all_gather | solution.py:110
  522.5 201.4 %all-gather.8.cloned.1.call-start = ((), (), s32[]{:S(2)}) async-start(), calls=%async_computation.6 | async-start | bytes 4128768 | tf_op jit(solution)/shard_map/all_gather | solution.py:104
  523.2 568.7 %reduce-scatter.14.cloned.1.call-start = ((), (), s32[]{:S(2)}) async-start(), calls=%async_computation.11 | async-start | bytes 2621440 | tf_op jit(solution)/shard_map/reduce_scatter | solution.py:119
  671.7 68.4 %copy-start.13 = (s32[1,1,56]{2,1,0:T(1,128)S(1)}, s32[1,1,56]{2,1,0:T(1,128)}, u32[]{:S(2)}) copy-start(s32[1,1,56]{2,1,0:T(1,128)} %param.16) | copy-start | bytes 676
  671.7 68.9 %copy-start.14 = (s32[1,1,56]{2,1,0:T(1,128)S(1)}, s32[1,1,56]{2,1,0:T(1,128)}, u32[]{:S(2)}) copy-start(s32[1,1,56]{2,1,0:T(1,128)} %param.19) | copy-start | bytes 676
  671.7 70.6 %copy-start.3 = (bf16[256,2048]{1,0:T(8,128)(2,1)S(1)}, bf16[256,2048]{1,0:T(8,128)(2,1)}, u32[]{:S(2)}) copy-start(bf16[256,2048]{1,0:T(8,128)(2,1)} %all-gather.10.cloned.1.call-done) | copy-start | bytes 3145732
  671.7 422.0 %reduce-scatter.12.cloned.1.call-start = ((), (), s32[]{:S(2)}) async-start(), calls=%async_computation.7 | async-start | bytes 2621440 | tf_op jit(solution)/shard_map/reduce_scatter | solution.py:118
  805.6 53.7 %copy-start.2 = (bf16[256,2048]{1,0:T(8,128)(2,1)S(1)}, bf16[256,2048]{1,0:T(8,128)(2,1)}, u32[]{:S(2)}) copy-start(bf16[256,2048]{1,0:T(8,128)(2,1)} %all-gather.6.cloned.1.call-done) | copy-start | bytes 3145732
  1076.4 6.8 copy-start.9
  1076.4 6.8 copy-start.11
  1083.2 3.9 copy-start
  1083.2 3.9 copy-start.5
  1083.2 3.9 copy-start.7
  1083.2 3.9 copy-start.10
  (3 other events, 1.8 us)
Sparse Core Ops, SparseCore 0:
  9.6 19.4 all-gather.9
  30.6 16.7 all-gather.5
  112.8 135.1 reduce-scatter.19
  251.4 131.7 reduce-scatter.15
  386.7 131.7 reduce-scatter.17
  521.9 65.8 all-gather.13
  590.6 65.2 all-gather.11
  658.6 65.2 all-gather.7
  726.4 29.8 reduce-scatter.13
  758.9 31.4 reduce-scatter.11
where the time goes:
time: 1110 us; the launch traced here: 1100 us
  local copies, waits for them, and re-layouts  505 us (45%)
  waiting for transfers between devices  384 us (35%)
  matrix products  173 us (16%)
  other arithmetic  24.7 us (2%)
  between operations  14.8 us (1%)
    unnamed x40, local copies, waits for them, and re-layouts  146 us
    reduce_scatter x1, waiting for transfers between devices, on_device(): lax.psum_scatter(up_part, 'col', scatter_dimension=0, tiled=True)  135 us
    reshape x3, local copies, waits for them, and re-layouts, block_grad(): dense.reshape(out_blocks, block_size, in_blocks, block_size)  135 us
    transpose x3, local copies, waits for them, and re-layouts, dense_matrix(): placed.reshape(out_blocks, in_blocks, block_size, block_size)  86.4 us
    reduce_scatter x1, waiting for transfers between devices, on_device(): lax.psum_scatter(gate_part, 'col', scatter_dimension=0, tiled=True)  76.4 us
    dot_general x3, matrix products, block_grad(): lax.dot_general(out_acts, in_acts, (((0,), (0,)), ((), ())), preferred_el...  68 us
    all_gather x1, waiting for transfers between devices, on_device(): lax.all_gather(up_piece, 'col', axis=0, tiled=True)  64.3 us
    slice x3, local copies, waits for them, and re-layouts, dense_matrix(): jnp.zeros((block_count + 1, block_size, block_size), jnp.bfloat16)  61.2 us
  transfers between devices with their start and end apart: 10, of which 5 were waited for; matrix products, arithmetic and copies ran while one was open for 63% of the time, Pallas kernels for 0%

commit v1 on v0

v1 whole, which is shorter than its diff:
```python
import functools

import jax
import jax.numpy as jnp
from jax import lax
from jax.experimental import pallas as pl
from jax.experimental.pallas import tpu as pltpu
from jax.sharding import PartitionSpec as P

FF_WIN = 28672
VMEM = pltpu.VMEM
SMEM = pltpu.SMEM


def scale_of(exponent):
    return jnp.where(exponent < 0, 0.5, jnp.where(exponent > 0, 2.0, 1.0)).astype(jnp.float32)


def scaled_block(values_ref, exps_ref, slot):
    scaled = values_ref[slot].astype(jnp.float32) * scale_of(exps_ref[slot])
    return scaled.astype(jnp.bfloat16)


def dot_nt(left, right):
    return lax.dot_general(left, right, (((1,), (1,)), ((), ())), preferred_element_type=jnp.float32)


def dot_nn(left, right):
    return lax.dot_general(left, right, (((1,), (0,)), ((), ())), preferred_element_type=jnp.float32)


def dot_tn(left, right):
    return lax.dot_general(left, right, (((0,), (0,)), ((), ())), preferred_element_type=jnp.float32)


def partial_kernel(
    pair_ids, down_ids, gate_exps, up_exps, down_exps,
    tokens, grads, gate_values, up_values, down_values,
    out, acc,
):
    slots, blk = gate_values.shape[0], gate_values.shape[1]
    width_blocks = tokens.shape[1] // blk
    hidden_blocks = acc.shape[0]
    count = hidden_blocks * width_blocks

    @pl.loop(0, hidden_blocks)
    def _(i):
        acc[i] = jnp.zeros(acc.shape[1:], jnp.float32)

    @pl.loop(0, slots)
    def _(s):
        pair = pair_ids[s]
        down = down_ids[s]

        @pl.when(pair < count)
        def _():
            i = pair // width_blocks
            j = pair % width_blocks
            cols = tokens[:, pl.ds(pl.multiple_of(j * blk, blk), blk)]
            weights = jnp.concatenate(
                [scaled_block(gate_values, gate_exps, s), scaled_block(up_values, up_exps, s)], axis=0
            )
            both = dot_nt(cols, weights)
            acc[i, 0] += both[:, :blk]
            acc[i, 1] += both[:, blk:]

        @pl.when(down < count)
        def _():
            i = down // hidden_blocks
            j = down % hidden_blocks
            cols = grads[:, pl.ds(pl.multiple_of(i * blk, blk), blk)]
            acc[j, 2] += dot_nn(cols, scaled_block(down_values, down_exps, s))

    @pl.loop(0, hidden_blocks)
    def _(i):
        out[i] = acc[i].astype(out.dtype)


def finish_kernel(
    pair_ids, down_ids, gate_exps, up_exps, down_exps,
    tokens, grads, gate_values, up_values, down_values, acts,
    parts, gate_grad, up_grad, down_grad,
):
    slots, blk = gate_values.shape[0], gate_values.shape[1]
    width_blocks = tokens.shape[1] // blk
    hidden_blocks = acts.shape[0]
    count = hidden_blocks * width_blocks

    parts[...] = jnp.zeros_like(parts)

    @pl.loop(0, slots)
    def _(s):
        pair = pair_ids[s]
        down = down_ids[s]

        @pl.when(pair < count)
        def _():
            i = pair // width_blocks
            j = pair % width_blocks
            at = pl.ds(pl.multiple_of(j * blk, blk), blk)
            cols = tokens[:, at]
            acts_both = jnp.concatenate([acts[i, 1], acts[i, 2]], axis=1)
            weights = jnp.concatenate(
                [scaled_block(gate_values, gate_exps, s), scaled_block(up_values, up_exps, s)], axis=0
            )
            parts[1, :, at] += dot_nn(acts_both, weights)
            both = dot_tn(acts_both, cols)
            gate_grad[s] = (both[:blk] * scale_of(gate_exps[s])).astype(jnp.bfloat16)
            up_grad[s] = (both[blk:] * scale_of(up_exps[s])).astype(jnp.bfloat16)

        @pl.when(pair >= count)
        def _():
            gate_grad[s] = jnp.zeros((blk, blk), jnp.bfloat16)
            up_grad[s] = jnp.zeros((blk, blk), jnp.bfloat16)

        @pl.when(down < count)
        def _():
            i = down // hidden_blocks
            j = down % hidden_blocks
            at = pl.ds(pl.multiple_of(i * blk, blk), blk)
            hidden = acts[j, 0]
            parts[0, :, at] += dot_nt(hidden, scaled_block(down_values, down_exps, s))
            grad = dot_tn(grads[:, at], hidden)
            down_grad[s] = (grad * scale_of(down_exps[s])).astype(jnp.bfloat16)

        @pl.when(down >= count)
        def _():
            down_grad[s] = jnp.zeros((blk, blk), jnp.bfloat16)


def derive(gate_sum, up_sum, hidden_grad):
    sigmoid_gate = jax.nn.sigmoid(gate_sum)
    silu = gate_sum * sigmoid_gate
    hidden = silu * up_sum
    gate_piece = hidden_grad * up_sum * sigmoid_gate * (1.0 + gate_sum * (1.0 - sigmoid_gate))
    up_piece = hidden_grad * silu
    return hidden, gate_piece, up_piece


def exchange_xla(partial):
    summed = lax.psum_scatter(partial, "col", scatter_dimension=2, tiled=True).astype(jnp.float32)
    acts = jnp.stack(derive(summed[:, 0], summed[:, 1], summed[:, 2]), axis=1).astype(jnp.bfloat16)
    return lax.all_gather(acts, "col", axis=2, tiled=True)


def activations(sums):
    return [part.astype(jnp.bfloat16) for part in derive(*sums)]


def exchange_kernel(
    n_z, step_blocks, ahead,
    partial, acts,
    own, from_x, from_left, from_right, to_left, to_right, stage,
    own_sem, x_send, x_recv, right_send, right_recv, left_send, left_recv, act_send, act_recv, keep_sem,
):
    col = lax.axis_index("col")
    z, x = col // 2, col % 2
    peer, right, left = z * 2 + (1 - x), col + 2, col - 2
    half = partial.shape[2] // 2
    steps = partial.shape[0] // step_blocks
    lag = n_z
    mine = pl.ds(pl.multiple_of(x * half, half), half)
    theirs = pl.ds(pl.multiple_of((1 - x) * half, half), half)

    def blocks(k):
        return pl.ds(k * step_blocks, step_blocks)

    def remote(src, dst, send, recv, target):
        return pltpu.make_async_remote_copy(
            src_ref=src, dst_ref=dst, send_sem=send, recv_sem=recv,
            device_id={"col": target}, device_id_type=pl.DeviceIdType.MESH,
        )

    def x_copy(k):
        return remote(partial.at[blocks(k), :, theirs], from_x.at[blocks(k)], x_send.at[k], x_recv.at[k], peer)

    def right_copy(k):
        return remote(to_right.at[blocks(k)], from_left.at[blocks(k)], right_send.at[k], right_recv.at[k], right)

    def left_copy(k):
        return remote(to_left.at[blocks(k)], from_right.at[blocks(k)], left_send.at[k], left_recv.at[k], left)

    def act_copy(k):
        return remote(stage.at[blocks(k)], acts.at[blocks(k), :, mine], act_send.at[k], act_recv.at[k], peer)

    def keep_copy(k):
        return pltpu.make_async_copy(stage.at[blocks(k)], acts.at[blocks(k), :, mine], keep_sem.at[k])

    barrier = pltpu.get_barrier_semaphore()

    def greet(target):
        pl.semaphore_signal(barrier, inc=1, device_id={"col": target}, device_id_type=pl.DeviceIdType.MESH)

    greet(peer)
    pl.when(z > 0)(lambda: greet(left))
    pl.when(z < n_z - 1)(lambda: greet(right))
    pl.semaphore_wait(barrier, 1 + (z > 0).astype(jnp.int32) + (z < n_z - 1).astype(jnp.int32))

    own_copy = pltpu.make_async_copy(partial.at[:, :, mine], own, own_sem)
    own_copy.start()
    for k in range(ahead):
        x_copy(k).start()
    own_copy.wait()

    def each_block(k, body):
        @pl.loop(0, step_blocks)
        def _(b):
            body(k * step_blocks + b)

    def add_pair(i):
        for u in range(3):
            total = own[i, u].astype(jnp.float32) + from_x[i, u].astype(jnp.float32)
            own[i, u] = total.astype(jnp.bfloat16)

    def forward(source, target):
        def body(i):
            for u in range(3):
                total = own[i, u].astype(jnp.float32) + source[i, u].astype(jnp.float32)
                target[i, u] = total.astype(jnp.bfloat16)
        return body

    def start_chain(target):
        def body(i):
            target[i] = own[i]
        return body

    def finish(sources):
        def body(i):
            sums = []
            for u in range(3):
                total = own[i, u].astype(jnp.float32)
                for source in sources:
                    total += source[i, u].astype(jnp.float32)
                sums.append(total)
            for u, part in enumerate(activations(sums)):
                stage[i, u] = part
        return body

    @pl.loop(0, steps + lag)
    def _(t):
        @pl.when(t + ahead < steps)
        def _():
            x_copy(t + ahead).start()

        @pl.when(t < steps)
        def _():
            x_copy(t).wait_recv()
            each_block(t, add_pair)

        r = t - z

        @pl.when((r >= 0) & (r < steps) & (z < n_z - 1))
        def _():
            @pl.when(z == 0)
            def _():
                each_block(r, start_chain(to_right))

            @pl.when(z > 0)
            def _():
                right_copy(r).wait_recv()
                each_block(r, forward(from_left, to_right))

            right_copy(r).start()

        l = t - (n_z - 1 - z)

        @pl.when((l >= 0) & (l < steps) & (z > 0))
        def _():
            @pl.when(z == n_z - 1)
            def _():
                each_block(l, start_chain(to_left))

            @pl.when(z < n_z - 1)
            def _():
                left_copy(l).wait_recv()
                each_block(l, forward(from_right, to_left))

            left_copy(l).start()

        f = t - lag

        @pl.when(f >= 0)
        def _():
            @pl.when(z == 0)
            def _():
                left_copy(f).wait_recv()
                each_block(f, finish([from_right]))

            @pl.when(z == n_z - 1)
            def _():
                right_copy(f).wait_recv()
                each_block(f, finish([from_left]))

            @pl.when((z > 0) & (z < n_z - 1))
            def _():
                each_block(f, finish([from_left, from_right]))

            act_copy(f).start()
            keep_copy(f).start()

    @pl.loop(0, steps)
    def _(k):
        x_copy(k).wait_send()
        pl.when(z < n_z - 1)(lambda: right_copy(k).wait_send())
        pl.when(z > 0)(lambda: left_copy(k).wait_send())
        act_copy(k).wait()
        keep_copy(k).wait()


def exchange(partial, n_col):
    blocks, units, total, blk = partial.shape
    step_blocks = 2
    steps = blocks // step_blocks
    buffer = pltpu.VMEM((blocks, units, total // 2, blk), jnp.bfloat16)
    sems = pltpu.SemaphoreType.DMA((steps,))
    return pl.pallas_call(
        functools.partial(exchange_kernel, n_col // 2, step_blocks, min(6, steps)),
        out_shape=jax.ShapeDtypeStruct(partial.shape, jnp.bfloat16),
        in_specs=[pl.BlockSpec(memory_space=pl.ANY)],
        out_specs=pl.BlockSpec(memory_space=pl.ANY),
        scratch_shapes=[buffer] * 7 + [pltpu.SemaphoreType.DMA(())] + [sems] * 9,
        compiler_params=pltpu.CompilerParams(
            collective_id=0, has_side_effects=True, vmem_limit_bytes=60 * 1024 * 1024
        ),
        name="exchange",
    )(partial)


def on_device(
    n_row, n_col,
    tokens, out_grad, gate_values, gate_exps, up_values, up_exps, gate_up_ids,
    down_values, down_exps, down_ids,
):
    blk = gate_values.shape[-1]
    slots = gate_values.shape[2]
    pair_slots, down_slots = gate_up_ids[0, 0], down_ids[0, 0]
    exps = (gate_exps[0, 0], up_exps[0, 0], down_exps[0, 0])
    values = (gate_values[0, 0], up_values[0, 0], down_values[0, 0])
    tokens_all = lax.all_gather(tokens, "row", axis=0, tiled=True)
    grads_all = lax.all_gather(out_grad, "row", axis=0, tiled=True)
    total, width = tokens_all.shape
    hidden_blocks = FF_WIN // n_row // blk
    smem = pl.BlockSpec(memory_space=SMEM)
    vmem = pl.BlockSpec(memory_space=VMEM)
    params = pltpu.CompilerParams(vmem_limit_bytes=60 * 1024 * 1024)
    partial = pl.pallas_call(
        partial_kernel,
        out_shape=jax.ShapeDtypeStruct((hidden_blocks, 3, total, blk), jnp.bfloat16),
        in_specs=[smem] * 5 + [vmem] * 5,
        out_specs=vmem,
        scratch_shapes=[pltpu.VMEM((hidden_blocks, 3, total, blk), jnp.float32)],
        compiler_params=params,
        name="partial_sums",
    )(pair_slots, down_slots, *exps, tokens_all, grads_all, *values)
    paired = (n_row, n_col) == (4, 8)
    acts = exchange(partial, n_col) if paired else exchange_xla(partial)
    grad_shape = jax.ShapeDtypeStruct((slots, blk, blk), jnp.bfloat16)
    parts, gate_grad, up_grad, down_grad = pl.pallas_call(
        finish_kernel,
        out_shape=(jax.ShapeDtypeStruct((2, total, width), jnp.float32), grad_shape, grad_shape, grad_shape),
        in_specs=[smem] * 5 + [vmem] * 6,
        out_specs=(vmem,) * 4,
        compiler_params=params,
        name="finish",
    )(pair_slots, down_slots, *exps, tokens_all, grads_all, *values, acts)
    rows = lax.psum_scatter(parts, "row", scatter_dimension=1, tiled=True)
    rows = rows.astype(jnp.bfloat16)
    return rows[0], rows[1], gate_grad[None, None], up_grad[None, None], down_grad[None, None]


def solution(mesh):
    lists = P("row", "col", None, None, None)
    ids = P("row", "col", None)
    in_specs = (P("row", "col"), P("row", "col"), lists, ids, lists, ids, ids, lists, ids, ids)
    out_specs = (P("row", "col"), P("row", "col"), lists, lists, lists)
    body = functools.partial(on_device, mesh.shape["row"], mesh.shape["col"])
    return jax.shard_map(body, mesh=mesh, in_specs=in_specs, out_specs=out_specs, check_vma=False)
```

time: 1110 us -> 392 us (0.35)
  local copies, waits for them, and re-layouts: 505 us -> 0.84 us
  waiting for transfers between devices: 384 us -> 98.7 us
  Pallas kernels: 0 us -> 280 us
  matrix products: 173 us -> 0 us
  other arithmetic: 24.7 us -> 1.28 us
    pallas_call x0 -> x3, Pallas kernels: none -> 280 us  [the longest x1 240 us: exchange(): pl.pallas_call(functools.partial(exchange_kernel, n_col // 2, step_blocks...]
    dot_general x9 -> x0, matrix products: 173 us -> none  [the longest x3 68 us: block_grad(): lax.dot_general(out_acts, in_acts, (((0,), (0,)), ((), ())), preferred_el...]
    reduce_scatter x5 -> x1, waiting for transfers between devices: 212 us -> 58.7 us  [on_device(): rows = lax.psum_scatter(parts, 'row', scatter_dimension=1, tiled=True)]
    unnamed x40 -> x0, local copies, waits for them, and re-layouts: 146 us -> none
    reshape x3 -> x0, local copies, waits for them, and re-layouts: 135 us -> none  [block_grad(): dense.reshape(out_blocks, block_size, in_blocks, block_size)]
    all_gather x5 -> x2, waiting for transfers between devices: 170 us -> 38.6 us  [the longest x1 20.3 us: on_device(): tokens_all = lax.all_gather(tokens, 'row', axis=0, tiled=True)]
    transpose x3 -> x0, local copies, waits for them, and re-layouts: 86.4 us -> none  [dense_matrix(): placed.reshape(out_blocks, in_blocks, block_size, block_size)]
    slice x3 -> x0, local copies, waits for them, and re-layouts: 61.2 us -> none  [dense_matrix(): jnp.zeros((block_count + 1, block_size, block_size), jnp.bfloat16)]
  transfers between devices with their start and end apart: 10 -> 3, of which waited for: 5 -> 3; matrix products, arithmetic and copies ran while one was open for 63% -> 0% of each run, Pallas kernels for 0% -> 0%
where the time goes in v1:
time: 392 us; the launch traced here: 395 us
  Pallas kernels  280 us (71%)
  waiting for transfers between devices  98.7 us (25%)
  between operations  13.8 us (4%)
    pallas_call x1, Pallas kernels, exchange(): pl.pallas_call(functools.partial(exchange_kernel, n_col // 2, step_blocks...  240 us
    reduce_scatter x1, waiting for transfers between devices, on_device(): rows = lax.psum_scatter(parts, 'row', scatter_dimension=1, tiled=True)  58.7 us
    pallas_call x1, Pallas kernels, on_device(): pl.pallas_call(finish_kernel, out_shape=(jax.ShapeDtypeStruct((2, total,...  21.8 us
    all_gather x1, waiting for transfers between devices, on_device(): tokens_all = lax.all_gather(tokens, 'row', axis=0, tiled=True)  20.3 us
    all_gather x1, waiting for transfers between devices, on_device(): grads_all = lax.all_gather(out_grad, 'row', axis=0, tiled=True)  18.3 us
    pallas_call x1, Pallas kernels, on_device(): pl.pallas_call(partial_kernel, out_shape=jax.ShapeDtypeStruct((hidden_blo...  18.2 us
  transfers between devices with their start and end apart: 3, of which 3 were waited for; matrix products, arithmetic and copies ran while one was open for 0% of the time, Pallas kernels for 0%

profile of v1, /device:TPU:0, one launch (start us, length us, event | category | flops | bytes accessed | tf_op | source)
XLA Modules:
  0.0 395.0 jit_solution(1973535482276959629)
XLA Ops:
  7.2 0.0 all-gather.3.cloned.1.call-start
  7.2 0.7 all-gather.3.cloned.1.call-update
  7.9 0.0 all-gather.5.cloned.1.call-start
  7.9 0.7 all-gather.5.cloned.1.call-update
  8.6 0.0 reduce-scatter.2.cloned.1.call-start
  8.7 20.3 %all-gather.3.cloned.1.call-done.tokens = bf16[256,2048]{1,0:T(8,128)(2,1)} async-done(((bf16[64,2048]{1,0:T(8,128)(2,1)}), bf16[256,2048]{1,0:T(8,128)(2,1)}) %all-gather.3.cloned.1.call-update) | async-done | bytes 1048592 | tf_op jit(solution)/shard_map/all_gather | solution.py:339
  29.0 18.3 %all-gather.5.cloned.1.call-done.grads = bf16[256,2048]{1,0:T(8,128)(2,1)} async-done(((bf16[64,2048]{1,0:T(8,128)(2,1)}), bf16[256,2048]{1,0:T(8,128)(2,1)}) %all-gather.5.cloned.1.call-update) | async-done | bytes 1048592 | tf_op jit(solution)/shard_map/all_gather | solution.py:340
  47.3 18.2 %partial_sums.1.partial = bf16[56,3,256,128]{3,2,1,0:T(8,128)(2,1)} custom-call(s32[56]{0:T(128)} %bitcast.21, s32[56]{0:T(128)} %bitcast.23, s32[56]{0:T(128)} %bitcast.25, s32[56]{0:T(128)} %bitcast.27, s32[56]{0:T(128)} %bitcast.29, bf16[256,2048]{1,0:T(8,128)(2,1)} %all-gather.3.cloned.1.call-done.tokens, ...), custom_call_target="tpu_custom_call" | custom-call | tf_op jit(solution)/shard_map/partial_sums/pallas_call | solution.py:346
  65.5 240.3 %exchange.1.acts = bf16[56,3,256,128]{3,2,1,0:T(8,128)(2,1)} custom-call(bf16[56,3,256,128]{3,2,1,0:T(8,128)(2,1)} %partial_sums.1.partial), custom_call_target="tpu_custom_call" | custom-call | tf_op jit(solution)/shard_map/exchange/pallas_call | solution.py:316
  305.8 21.8 %finish.1 = (f32[2,256,2048]{2,1,0:T(8,128)}, bf16[56,128,128]{2,1,0:T(8,128)(2,1)}, bf16[56,128,128]{2,1,0:T(8,128)(2,1)}, bf16[56,128,128]{2,1,0:T(8,128)(2,1)}) custom-call(s32[56]{0:T(128)} %bitcast.22, s32[56]{0:T(128)} %bitcast.24, s32[56]{0:T(128)} %bitcast.26, s32[56]{0:T(128)} %bitcast.28, s32[56]{0:T(128)} %bitcast.30, ...), custom_call_target="tpu_custom_call" | custom-call | tf_op jit(solution)/shard_map/finish/pallas_call | solution.py:358
  327.6 0.0 reduce-scatter.2.cloned.1.call-update
  327.6 58.7 %reduce-scatter.2.cloned.1.call-done = f32[2,64,2048]{2,1,0:T(8,128)} async-done(((f32[2,256,2048]{2,1,0:T(8,128)}), f32[2,64,2048]{2,1,0:T(8,128)}) %reduce-scatter.2.cloned.1.call-update) | async-done | bytes 1048592 | tf_op jit(solution)/shard_map/reduce_scatter | solution.py:366
  386.3 1.3 convert_element_type.3
  387.6 0.8 slice_bitcast_fusion
Async XLA Ops:
  7.2 21.9 %all-gather.3.cloned.1.call-start = ((), (), s32[]{:S(2)}) async-start(), calls=%async_computation.1 | async-start | bytes 1310720 | tf_op jit(solution)/shard_map/all_gather | solution.py:339
  7.9 39.4 %all-gather.5.cloned.1.call-start = ((), (), s32[]{:S(2)}) async-start(), calls=%async_computation.2 | async-start | bytes 1310720 | tf_op jit(solution)/shard_map/all_gather | solution.py:340
  8.6 377.7 %reduce-scatter.2.cloned.1.call-start = ((), (), s32[]{:S(2)}) async-start(), calls=%async_computation.3 | async-start | bytes 5242880 | tf_op jit(solution)/shard_map/reduce_scatter | solution.py:366
Sparse Core Ops, SparseCore 0:
  9.6 19.4 all-gather.2
  30.6 16.7 all-gather.4
  327.7 58.5 reduce-scatter.1

commit v2 on v1

--- a/solution.py
+++ b/solution.py
@@ -36,8 +36,9 @@
 def partial_kernel(
     pair_ids, down_ids, gate_exps, up_exps, down_exps,
     tokens, grads, gate_values, up_values, down_values,
-    out, acc,
+    *rest,
 ):
+    acc = rest[-1]
     slots, blk = gate_values.shape[0], gate_values.shape[1]
     width_blocks = tokens.shape[1] // blk
     hidden_blocks = acc.shape[0]
@@ -71,9 +72,25 @@
             cols = grads[:, pl.ds(pl.multiple_of(i * blk, blk), blk)]
             acc[j, 2] += dot_nn(cols, scaled_block(down_values, down_exps, s))
 
-    @pl.loop(0, hidden_blocks)
-    def _(i):
-        out[i] = acc[i].astype(out.dtype)
+    if len(rest) == 2:
+        @pl.loop(0, hidden_blocks)
+        def _(i):
+            rest[0][i] = acc[i].astype(rest[0].dtype)
+    else:
+        sent, own, full = rest[:3]
+        paired, half = own.shape[0], own.shape[2]
+        x = lax.axis_index("col") % 2
+        mine = pl.ds(pl.multiple_of(x * half, half), half)
+        theirs = pl.ds(pl.multiple_of((1 - x) * half, half), half)
+
+        @pl.loop(0, paired)
+        def _(i):
+            sent[i] = acc[i, :, theirs].astype(sent.dtype)
+            own[i] = acc[i, :, mine]
+
+        @pl.loop(paired, hidden_blocks)
+        def _(i):
+            full[i - paired] = acc[i]
 
 
 def finish_kernel(
@@ -148,22 +165,24 @@
 
 
 def exchange_kernel(
-    n_z, step_blocks, ahead,
-    partial, acts,
+    n_z, ahead,
+    sent, own_in, full_in, acts,
     own, from_x, from_left, from_right, to_left, to_right, stage,
-    own_sem, x_send, x_recv, right_send, right_recv, left_send, left_recv, act_send, act_recv, keep_sem,
+    full, in_left, in_right, chain, pair_out, pair_in, joined,
+    load_sem, a_send, a_recv, b_send, b_recv, pair_send, pair_recv, keep_sem, out_sem,
 ):
     col = lax.axis_index("col")
     z, x = col // 2, col % 2
     peer, right, left = z * 2 + (1 - x), col + 2, col - 2
-    half = partial.shape[2] // 2
-    steps = partial.shape[0] // step_blocks
-    lag = n_z
+    last = n_z - 1
+    half = own.shape[2]
+    quarter = full.shape[2] // n_z
+    n_a, n_b = own.shape[0], full.shape[0]
     mine = pl.ds(pl.multiple_of(x * half, half), half)
-    theirs = pl.ds(pl.multiple_of((1 - x) * half, half), half)
-
-    def blocks(k):
-        return pl.ds(k * step_blocks, step_blocks)
+    my_quarter = pl.ds(pl.multiple_of(z * quarter, quarter), quarter)
+
+    def rows(d):
+        return pl.ds(d * quarter, quarter)
 
     def remote(src, dst, send, recv, target):
         return pltpu.make_async_remote_copy(
@@ -172,19 +191,37 @@
         )
 
     def x_copy(k):
-        return remote(partial.at[blocks(k), :, theirs], from_x.at[blocks(k)], x_send.at[k], x_recv.at[k], peer)
+        return remote(sent.at[k], from_x.at[k], a_send.at[0, k], a_recv.at[0, k], peer)
 
     def right_copy(k):
-        return remote(to_right.at[blocks(k)], from_left.at[blocks(k)], right_send.at[k], right_recv.at[k], right)
+        return remote(to_right.at[k], from_left.at[k], a_send.at[1, k], a_recv.at[1, k], right)
 
     def left_copy(k):
-        return remote(to_left.at[blocks(k)], from_right.at[blocks(k)], left_send.at[k], left_recv.at[k], left)
+        return remote(to_left.at[k], from_right.at[k], a_send.at[2, k], a_recv.at[2, k], left)
 
     def act_copy(k):
-        return remote(stage.at[blocks(k)], acts.at[blocks(k), :, mine], act_send.at[k], act_recv.at[k], peer)
+        return remote(stage.at[k], acts.at[k, :, mine], a_send.at[3, k], a_recv.at[3, k], peer)
 
     def keep_copy(k):
-        return pltpu.make_async_copy(stage.at[blocks(k)], acts.at[blocks(k), :, mine], keep_sem.at[k])
+        return pltpu.make_async_copy(stage.at[k], acts.at[k, :, mine], keep_sem.at[k])
+
+    def chain_right(k, d):
+        return remote(chain.at[k, :, rows(d)], in_left.at[k, :, rows(d)], b_send.at[0, d, k], b_recv.at[0, d, k], right)
+
+    def chain_left(k, d):
+        return remote(chain.at[k, :, rows(d)], in_right.at[k, :, rows(d)], b_send.at[1, d, k], b_recv.at[1, d, k], left)
+
+    def pair_copy(k):
+        return remote(pair_out.at[k], pair_in.at[k], pair_send.at[k], pair_recv.at[k], peer)
+
+    def gather_right(k, d):
+        return remote(joined.at[k, :, rows(d)], joined.at[k, :, rows(d)], b_send.at[2, d, k], b_recv.at[2, d, k], right)
+
+    def gather_left(k, d):
+        return remote(joined.at[k, :, rows(d)], joined.at[k, :, rows(d)], b_send.at[3, d, k], b_recv.at[3, d, k], left)
+
+    def out_copy(k):
+        return pltpu.make_async_copy(joined.at[k], acts.at[n_a + k], out_sem.at[k])
 
     barrier = pltpu.get_barrier_semaphore()
 
@@ -193,137 +230,373 @@
 
     greet(peer)
     pl.when(z > 0)(lambda: greet(left))
-    pl.when(z < n_z - 1)(lambda: greet(right))
-    pl.semaphore_wait(barrier, 1 + (z > 0).astype(jnp.int32) + (z < n_z - 1).astype(jnp.int32))
-
-    own_copy = pltpu.make_async_copy(partial.at[:, :, mine], own, own_sem)
-    own_copy.start()
-    for k in range(ahead):
+    pl.when(z < last)(lambda: greet(right))
+    pl.semaphore_wait(barrier, 1 + (z > 0).astype(jnp.int32) + (z < last).astype(jnp.int32))
+
+    own_load = pltpu.make_async_copy(own_in, own, load_sem.at[0])
+    full_load = pltpu.make_async_copy(full_in, full, load_sem.at[1])
+    for k in range(min(ahead, n_a)):
         x_copy(k).start()
-    own_copy.wait()
-
-    def each_block(k, body):
-        @pl.loop(0, step_blocks)
-        def _(b):
-            body(k * step_blocks + b)
-
-    def add_pair(i):
+    full_load.start()
+    own_load.start()
+    full_load.wait()
+    own_load.wait()
+
+    def f32(value):
+        return value.astype(jnp.float32)
+
+    def join(k, target, sources):
         for u in range(3):
-            total = own[i, u].astype(jnp.float32) + from_x[i, u].astype(jnp.float32)
-            own[i, u] = total.astype(jnp.bfloat16)
-
-    def forward(source, target):
-        def body(i):
-            for u in range(3):
-                total = own[i, u].astype(jnp.float32) + source[i, u].astype(jnp.float32)
-                target[i, u] = total.astype(jnp.bfloat16)
-        return body
-
-    def start_chain(target):
-        def body(i):
-            target[i] = own[i]
-        return body
-
-    def finish(sources):
-        def body(i):
-            sums = []
-            for u in range(3):
-                total = own[i, u].astype(jnp.float32)
-                for source in sources:
-                    total += source[i, u].astype(jnp.float32)
-                sums.append(total)
-            for u, part in enumerate(activations(sums)):
-                stage[i, u] = part
-        return body
-
-    @pl.loop(0, steps + lag)
-    def _(t):
-        @pl.when(t + ahead < steps)
-        def _():
-            x_copy(t + ahead).start()
-
-        @pl.when(t < steps)
+            total = own[k, u]
+            for source in sources:
+                total += f32(source[k, u])
+            target[k, u] = total.astype(target.dtype)
+
+    def finish(k, sources):
+        sums = []
+        for u in range(3):
+            total = own[k, u]
+            for source in sources:
+                total += f32(source[k, u])
+            sums.append(total)
+        for u, part in enumerate(activations(sums)):
+            stage[k, u] = part
+
+    def paired_step(t):
+        @pl.when(t < n_a)
         def _():
             x_copy(t).wait_recv()
-            each_block(t, add_pair)
+            join(t, own, [from_x])
 
         r = t - z
 
-        @pl.when((r >= 0) & (r < steps) & (z < n_z - 1))
+        @pl.when((r >= 0) & (r < n_a) & (z < last))
         def _():
             @pl.when(z == 0)
             def _():
-                each_block(r, start_chain(to_right))
+                join(r, to_right, [])
 
             @pl.when(z > 0)
             def _():
                 right_copy(r).wait_recv()
-                each_block(r, forward(from_left, to_right))
+                join(r, to_right, [from_left])
 
             right_copy(r).start()
 
-        l = t - (n_z - 1 - z)
-
-        @pl.when((l >= 0) & (l < steps) & (z > 0))
-        def _():
-            @pl.when(z == n_z - 1)
-            def _():
-                each_block(l, start_chain(to_left))
-
-            @pl.when(z < n_z - 1)
+        l = t - (last - z)
+
+        @pl.when((l >= 0) & (l < n_a) & (z > 0))
+        def _():
+            @pl.when(z == last)
+            def _():
+                join(l, to_left, [])
+
+            @pl.when(z < last)
             def _():
                 left_copy(l).wait_recv()
-                each_block(l, forward(from_right, to_left))
+                join(l, to_left, [from_right])
 
             left_copy(l).start()
 
-        f = t - lag
-
-        @pl.when(f >= 0)
+        f = t - n_z
+
+        @pl.when((f >= 0) & (f < n_a))
         def _():
             @pl.when(z == 0)
             def _():
                 left_copy(f).wait_recv()
-                each_block(f, finish([from_right]))
-
-            @pl.when(z == n_z - 1)
+                finish(f, [from_right])
+
+            @pl.when(z == last)
             def _():
                 right_copy(f).wait_recv()
-                each_block(f, finish([from_left]))
-
-            @pl.when((z > 0) & (z < n_z - 1))
-            def _():
-                each_block(f, finish([from_left, from_right]))
+                finish(f, [from_left])
+
+            @pl.when((z > 0) & (z < last))
+            def _():
+                finish(f, [from_left, from_right])
 
             act_copy(f).start()
             keep_copy(f).start()
 
-    @pl.loop(0, steps)
+    def join_rows(k, d, sources):
+        for u in range(3):
+            total = full[k, u, rows(d)]
+            for source in sources:
+                total += f32(source[k, u, rows(d)])
+            chain[k, u, rows(d)] = total.astype(chain.dtype)
+
+    def chain_step(t):
+        r = t - z
+
+        @pl.when((r >= 0) & (r < n_b))
+        def _():
+            for d in range(1, n_z):
+                @pl.when(d > z)
+                def _():
+                    @pl.when(z == 0)
+                    def _():
+                        join_rows(r, d, [])
+
+                    @pl.when(z > 0)
+                    def _():
+                        chain_right(r, d).wait_recv()
+                        join_rows(r, d, [in_left])
+
+                    chain_right(r, d).start()
+
+        l = t - (last - z)
+
+        @pl.when((l >= 0) & (l < n_b))
+        def _():
+            for d in range(last):
+                @pl.when(d < z)
+                def _():
+                    @pl.when(z == last)
+                    def _():
+                        join_rows(l, d, [])
+
+                    @pl.when(z < last)
+                    def _():
+                        chain_left(l, d).wait_recv()
+                        join_rows(l, d, [in_right])
+
+                    chain_left(l, d).start()
+
+        f = t - n_z
+
+        @pl.when((f >= 0) & (f < n_b))
+        def _():
+            def add_mine(source):
+                for u in range(3):
+                    full[f, u, my_quarter] += f32(source[f, u, my_quarter])
+
+            @pl.when(z > 0)
+            def _():
+                chain_right(f, z).wait_recv()
+                add_mine(in_left)
+
+            @pl.when(z < last)
+            def _():
+                chain_left(f, z).wait_recv()
+                add_mine(in_right)
+
+            pair_out[f] = full[f, :, my_quarter].astype(pair_out.dtype)
+            pair_copy(f).start()
+
+        g = t - n_z - 2
+
+        @pl.when((g >= 0) & (g < n_b))
+        def _():
+            pair_copy(g).wait_recv()
+            sums = [full[g, u, my_quarter] + f32(pair_in[g, u]) for u in range(3)]
+            for u, part in enumerate(activations(sums)):
+                joined[g, u, my_quarter] = part
+            pl.when(z < last)(lambda: gather_right(g, z).start())
+            pl.when(z > 0)(lambda: gather_left(g, z).start())
+
+        for d in range(n_z):
+            right_at = g - (z - d)
+            left_at = g - (d - z)
+
+            @pl.when((d < z) & (right_at >= 0) & (right_at < n_b))
+            def _():
+                gather_right(right_at, d).wait_recv()
+                pl.when(z < last)(lambda: gather_right(right_at, d).start())
+
+            @pl.when((d > z) & (left_at >= 0) & (left_at < n_b))
+            def _():
+                gather_left(left_at, d).wait_recv()
+                pl.when(z > 0)(lambda: gather_left(left_at, d).start())
+
+        done = g - last
+
+        @pl.when((done >= 0) & (done < n_b))
+        def _():
+            out_copy(done).start()
+
+    @pl.loop(0, max(n_a + n_z, n_b + n_z + 2 + last) + 1)
+    def _(t):
+        first = ahead + t + (t + 1) // 2
+
+        @pl.when(first < n_a)
+        def _():
+            x_copy(first).start()
+
+        @pl.when((t % 2 == 0) & (first + 1 < n_a))
+        def _():
+            x_copy(first + 1).start()
+
+        chain_step(t)
+        paired_step(t)
+
+    @pl.loop(0, n_a)
     def _(k):
         x_copy(k).wait_send()
-        pl.when(z < n_z - 1)(lambda: right_copy(k).wait_send())
+        pl.when(z < last)(lambda: right_copy(k).wait_send())
         pl.when(z > 0)(lambda: left_copy(k).wait_send())
         act_copy(k).wait()
         keep_copy(k).wait()
 
-
-def exchange(partial, n_col):
-    blocks, units, total, blk = partial.shape
-    step_blocks = 2
-    steps = blocks // step_blocks
-    buffer = pltpu.VMEM((blocks, units, total // 2, blk), jnp.bfloat16)
-    sems = pltpu.SemaphoreType.DMA((steps,))
+    @pl.loop(0, n_b)
+    def _(k):
+        pair_copy(k).wait_send()
+        out_copy(k).wait()
+        for d in range(n_z):
+            pl.when(d > z)(lambda: chain_right(k, d).wait_send())
+            pl.when(d < z)(lambda: chain_left(k, d).wait_send())
+            pl.when((d <= z) & (z < last))(lambda: gather_right(k, d).wait_send())
+            pl.when((d >= z) & (z > 0))(lambda: gather_left(k, d).wait_send())
+
+
+def exchange(sent, own, full, n_col):
+    n_a, units, half, blk = own.shape
+    n_b, total = full.shape[0], full.shape[2]
+    n_z = n_col // 2
+    bf16 = jnp.bfloat16
+    halves = pltpu.VMEM((n_a, units, half, blk), bf16)
+    wholes = pltpu.VMEM((n_b, units, total, blk), bf16)
+    quarters = pltpu.VMEM((n_b, units, total // n_z, blk), bf16)
+    dma = pltpu.SemaphoreType.DMA
+    anywhere = pl.BlockSpec(memory_space=pl.ANY)
     return pl.pallas_call(
-        functools.partial(exchange_kernel, n_col // 2, step_blocks, min(6, steps)),
-        out_shape=jax.ShapeDtypeStruct(partial.shape, jnp.bfloat16),
-        in_specs=[pl.BlockSpec(memory_space=pl.ANY)],
-        out_specs=pl.BlockSpec(memory_space=pl.ANY),
-        scratch_shapes=[buffer] * 7 + [pltpu.SemaphoreType.DMA(())] + [sems] * 9,
+        functools.partial(exchange_kernel, n_z, min(4, n_a)),
+        out_shape=jax.ShapeDtypeStruct((n_a + n_b, units, total, blk), bf16),
+        in_specs=[anywhere] * 3,
+        out_specs=anywhere,
+        scratch_shapes=[pltpu.VMEM(own.shape, jnp.float32)] + [halves] * 6
+        + [pltpu.VMEM(full.shape, jnp.float32)] + [wholes] * 3 + [quarters] * 2 + [wholes]
+        + [dma((2,)), dma((4, n_a)), dma((4, n_a)), dma((4, n_z, n_b)), dma((4, n_z, n_b))]
+        + [dma((n_b,)), dma((n_b,)), dma((n_a,)), dma((n_b,))],
         compiler_params=pltpu.CompilerParams(
             collective_id=0, has_side_effects=True, vmem_limit_bytes=60 * 1024 * 1024
         ),
         name="exchange",
-    )(partial)
+    )(sent, own, full)
+
+
+def row_neighbours():
+    row = lax.axis_index("row")
+    y, core = row // 2, row % 2
+    return row, y, core, (1 - y) * 2 + core, y * 2 + (1 - core)
+
+
+def row_remote(src, dst, send, recv, target):
+    return pltpu.make_async_remote_copy(
+        src_ref=src, dst_ref=dst, send_sem=send, recv_sem=recv,
+        device_id={"row": target}, device_id_type=pl.DeviceIdType.MESH,
+    )
+
+
+def row_barrier(targets):
+    barrier = pltpu.get_barrier_semaphore()
+    for target in targets:
+        pl.semaphore_signal(barrier, inc=1, device_id={"row": target}, device_id_type=pl.DeviceIdType.MESH)
+    pl.semaphore_wait(barrier, len(targets))
+
+
+def gather_kernel(tokens, grads, tokens_all, grads_all, send, recv, keep):
+    row, y, core, far, near = row_neighbours()
+    share = tokens.shape[0]
+    row_barrier((far, near))
+
+    def rows(index):
+        return pl.ds(pl.multiple_of(index * share, share), share)
+
+    pairs = ((tokens, tokens_all), (grads, grads_all))
+    across = [row_remote(src, dst.at[rows(row)], send.at[0, a], recv.at[0, a], far) for a, (src, dst) in enumerate(pairs)]
+    beside = [row_remote(src, dst.at[rows(row)], send.at[1, a], recv.at[1, a], near) for a, (src, dst) in enumerate(pairs)]
+    onward = [
+        row_remote(dst.at[rows(far)], dst.at[rows(far)], send.at[2, a], recv.at[2, a], near)
+        for a, (src, dst) in enumerate(pairs)
+    ]
+    local = [pltpu.make_async_copy(src, dst.at[rows(row)], keep.at[a]) for a, (src, dst) in enumerate(pairs)]
+    for copy in across + beside + local:
+        copy.start()
+    for a in range(2):
+        across[a].wait_recv()
+        onward[a].start()
+    for a in range(2):
+        across[a].wait_send()
+        beside[a].wait()
+        onward[a].wait()
+        local[a].wait()
+
+
+def gather_rows(tokens, grads, n_row):
+    whole = jax.ShapeDtypeStruct((tokens.shape[0] * n_row, tokens.shape[1]), tokens.dtype)
+    anywhere = pl.BlockSpec(memory_space=pl.ANY)
+    dma = pltpu.SemaphoreType.DMA
+    return pl.pallas_call(
+        gather_kernel,
+        out_shape=(whole, whole),
+        in_specs=[anywhere] * 2,
+        out_specs=(anywhere,) * 2,
+        scratch_shapes=[dma((3, 2)), dma((3, 2)), dma((2,))],
+        compiler_params=pltpu.CompilerParams(collective_id=1, has_side_effects=True),
+        name="gather_rows",
+    )(tokens, grads)
+
+
+def sum_kernel(parts, output, input_grad, from_near, to_far, from_far, send, recv):
+    row, y, core, far, near = row_neighbours()
+    share = output.shape[0]
+    results = (output, input_grad)
+    row_barrier((far, near))
+
+    def rows(index):
+        return pl.ds(pl.multiple_of(index * share, share), share)
+
+    def near_copy(place, u):
+        index = jnp.where(place == 0, 1 - y, y) * 2 + (1 - core)
+        return row_remote(
+            parts.at[u, rows(index)], from_near.at[place, u], send.at[place, u], recv.at[place, u], near
+        )
+
+    def far_copy(u):
+        return row_remote(to_far.at[u], from_far.at[u], send.at[2, u], recv.at[2, u], far)
+
+    for place in range(2):
+        for u in range(2):
+            near_copy(place, u).start()
+    for u in range(2):
+        near_copy(0, u).wait_recv()
+        to_far[u] = (parts[u, rows(far)] + from_near[0, u]).astype(to_far.dtype)
+        far_copy(u).start()
+    for u in range(2):
+        near_copy(1, u).wait_recv()
+        from_near[1, u] += parts[u, rows(row)]
+    for u in range(2):
+        far_copy(u).wait_recv()
+        results[u][...] = (from_near[1, u] + from_far[u].astype(jnp.float32)).astype(jnp.bfloat16)
+    for u in range(2):
+        near_copy(0, u).wait_send()
+        near_copy(1, u).wait_send()
+        far_copy(u).wait_send()
+
+
+def sum_rows(parts, n_row):
+    units, total, width = parts.shape
+    share = total // n_row
+    result = jax.ShapeDtypeStruct((share, width), jnp.bfloat16)
+    vmem = pl.BlockSpec(memory_space=VMEM)
+    dma = pltpu.SemaphoreType.DMA
+    return pl.pallas_call(
+        sum_kernel,
+        out_shape=(result, result),
+        in_specs=[vmem],
+        out_specs=(vmem, vmem),
+        scratch_shapes=[
+            pltpu.VMEM((2, units, share, width), jnp.float32),
+            pltpu.VMEM((units, share, width), jnp.bfloat16),
+            pltpu.VMEM((units, share, width), jnp.bfloat16),
+            dma((3, units)), dma((3, units)),
+        ],
+        compiler_params=pltpu.CompilerParams(
+            collective_id=2, has_side_effects=True, vmem_limit_bytes=32 * 1024 * 1024
+        ),
+        name="sum_rows",
+    )(parts)
 
 
 def on_device(
@@ -336,24 +609,37 @@
     pair_slots, down_slots = gate_up_ids[0, 0], down_ids[0, 0]
     exps = (gate_exps[0, 0], up_exps[0, 0], down_exps[0, 0])
     values = (gate_values[0, 0], up_values[0, 0], down_values[0, 0])
-    tokens_all = lax.all_gather(tokens, "row", axis=0, tiled=True)
-    grads_all = lax.all_gather(out_grad, "row", axis=0, tiled=True)
+    paired = (n_row, n_col) == (4, 8)
+    if paired:
+        tokens_all, grads_all = gather_rows(tokens, out_grad, n_row)
+    else:
+        tokens_all = lax.all_gather(tokens, "row", axis=0, tiled=True)
+        grads_all = lax.all_gather(out_grad, "row", axis=0, tiled=True)
     total, width = tokens_all.shape
     hidden_blocks = FF_WIN // n_row // blk
     smem = pl.BlockSpec(memory_space=SMEM)
     vmem = pl.BlockSpec(memory_space=VMEM)
     params = pltpu.CompilerParams(vmem_limit_bytes=60 * 1024 * 1024)
+    if paired:
+        n_a = hidden_blocks * 17 // 28
+        half = (n_a, 3, total // 2, blk)
+        partial_shape = (
+            jax.ShapeDtypeStruct(half, jnp.bfloat16),
+            jax.ShapeDtypeStruct(half, jnp.float32),
+            jax.ShapeDtypeStruct((hidden_blocks - n_a, 3, total, blk), jnp.float32),
+        )
+    else:
+        partial_shape = (jax.ShapeDtypeStruct((hidden_blocks, 3, total, blk), jnp.bfloat16),)
     partial = pl.pallas_call(
         partial_kernel,
-        out_shape=jax.ShapeDtypeStruct((hidden_blocks, 3, total, blk), jnp.bfloat16),
+        out_shape=partial_shape,
         in_specs=[smem] * 5 + [vmem] * 5,
-        out_specs=vmem,
+        out_specs=(vmem,) * len(partial_shape),
         scratch_shapes=[pltpu.VMEM((hidden_blocks, 3, total, blk), jnp.float32)],
         compiler_params=params,
         name="partial_sums",
     )(pair_slots, down_slots, *exps, tokens_all, grads_all, *values)
-    paired = (n_row, n_col) == (4, 8)
-    acts = exchange(partial, n_col) if paired else exchange_xla(partial)
+    acts = exchange(*partial, n_col) if paired else exchange_xla(partial[0])
     grad_shape = jax.ShapeDtypeStruct((slots, blk, blk), jnp.bfloat16)
     parts, gate_grad, up_grad, down_grad = pl.pallas_call(
         finish_kernel,
@@ -363,8 +649,10 @@
         compiler_params=params,
         name="finish",
     )(pair_slots, down_slots, *exps, tokens_all, grads_all, *values, acts)
-    rows = lax.psum_scatter(parts, "row", scatter_dimension=1, tiled=True)
-    rows = rows.astype(jnp.bfloat16)
+    if paired:
+        rows = sum_rows(parts, n_row)
+    else:
+        rows = lax.psum_scatter(parts, "row", scatter_dimension=1, tiled=True).astype(jnp.bfloat16)
     return rows[0], rows[1], gate_grad[None, None], up_grad[None, None], down_grad[None, None]
 
 

time: 392 us -> 303 us (0.77); the launches traced: 395 us -> 298 us
  waiting for transfers between devices: 98.7 us -> 0 us
  between operations: 13.8 us -> 0.66 us
  Pallas kernels: 280 us -> 293 us
    reduce_scatter x1 -> x0, waiting for transfers between devices: 58.7 us -> none  [on_device(): rows = lax.psum_scatter(parts, 'row', scatter_dimension=1, tiled=True)]
    all_gather x2 -> x0, waiting for transfers between devices: 38.6 us -> none  [the longest x1 20.3 us: on_device(): tokens_all = lax.all_gather(tokens, 'row', axis=0, tiled=True)]
    pallas_call x2 -> x4, Pallas kernels: 258 us -> 272 us  [the longest x1 217 us: exchange(): pl.pallas_call(functools.partial(exchange_kernel, n_z, min(4, n_a)), out_...]
  transfers between devices with their start and end apart: 3 -> 0, of which waited for: 3 -> 0; matrix products, arithmetic and copies ran while one was open for 0% -> 0% of each run, Pallas kernels for 0% -> 0%
where the time goes in v2:
time: 303 us; the launch traced here: 298 us
  Pallas kernels  293 us (97%)
  local copies, waits for them, and re-layouts  3.59 us (1%)
    pallas_call x1, Pallas kernels, exchange(): pl.pallas_call(functools.partial(exchange_kernel, n_z, min(4, n_a)), out_...  217 us
    pallas_call x1, Pallas kernels, on_device(): pl.pallas_call(finish_kernel, out_shape=(jax.ShapeDtypeStruct((2, total,...  21.8 us
    pallas_call x1, Pallas kernels, on_device(): pl.pallas_call(partial_kernel, out_shape=partial_shape, in_specs=[smem] *...  21 us
    pallas_call x1, Pallas kernels, gather_rows(): pl.pallas_call(gather_kernel, out_shape=(whole, whole), in_specs=[anywher...  20.1 us
    pallas_call x1, Pallas kernels, sum_rows(): pl.pallas_call(sum_kernel, out_shape=(result, result), in_specs=[vmem], o...  13.8 us

profile of v2, /device:TPU:0, one launch (start us, length us, event | category | flops | bytes accessed | tf_op | source)
XLA Modules:
  0.0 297.6 jit_solution(11841777897054436804)
XLA Ops:
  0.6 20.1 %gather_rows.1 = (bf16[256,2048]{1,0:T(8,128)(2,1)}, bf16[256,2048]{1,0:T(8,128)(2,1)}) custom-call(bf16[64,2048]{1,0:T(8,128)(2,1)} %tokens.1, bf16[64,2048]{1,0:T(8,128)(2,1)} %grads.1), custom_call_target="tpu_custom_call" | custom-call | tf_op jit(solution)/shard_map/gather_rows/pallas_call | solution.py:530
  20.8 21.0 %partial_sums.1 = (bf16[34,3,128,128]{3,2,1,0:T(8,128)(2,1)}, f32[34,3,128,128]{3,2,1,0:T(8,128)}, f32[22,3,256,128]{3,2,1,0:T(8,128)}) custom-call(s32[56]{0:T(128)} %bitcast.17, s32[56]{0:T(128)} %bitcast.19, s32[56]{0:T(128)} %bitcast.21, s32[56]{0:T(128)} %bitcast.23, s32[56]{0:T(128)} %bitcast.25, bf16[256,2048]{1,0:T(8,128)(2,1)} %get-tuple-element.16.tokens, ...), custom_call_target="tpu_custom_call" | custom-call | tf_op jit(solution)/shard_map/partial_sums/pallas_call | solution.py:633
  41.8 216.7 %exchange.1.acts = bf16[56,3,256,128]{3,2,1,0:T(8,128)(2,1)} custom-call(bf16[34,3,128,128]{3,2,1,0:T(8,128)(2,1)} %get-tuple-element.18.sent, f32[34,3,128,128]{3,2,1,0:T(8,128)} %get-tuple-element.19.own_in, f32[22,3,256,128]{3,2,1,0:T(8,128)} %get-tuple-element.20.full_in), custom_call_target="tpu_custom_call" | custom-call | tf_op jit(solution)/shard_map/exchange/pallas_call | solution.py:462
  258.4 21.8 %finish.1 = (f32[2,256,2048]{2,1,0:T(8,128)}, bf16[56,128,128]{2,1,0:T(8,128)(2,1)}, bf16[56,128,128]{2,1,0:T(8,128)(2,1)}, bf16[56,128,128]{2,1,0:T(8,128)(2,1)}) custom-call(s32[56]{0:T(128)} %bitcast.18, s32[56]{0:T(128)} %bitcast.20, s32[56]{0:T(128)} %bitcast.22, s32[56]{0:T(128)} %bitcast.24, s32[56]{0:T(128)} %bitcast.26, ...), custom_call_target="tpu_custom_call" | custom-call | tf_op jit(solution)/shard_map/finish/pallas_call | solution.py:644
  280.2 0.0 copy-start
  280.2 2.2 copy-done
  282.4 13.8 %sum_rows.1 = (bf16[64,2048]{1,0:T(8,128)(2,1)S(1)}, bf16[64,2048]{1,0:T(8,128)(2,1)S(1)}) custom-call(f32[2,256,2048]{2,1,0:T(8,128)S(1)} %copy-done), custom_call_target="tpu_custom_call" | custom-call | tf_op jit(solution)/shard_map/sum_rows/pallas_call | solution.py:584
  296.2 0.7 copy.17
  296.9 0.7 copy.18
Async XLA Ops:
  280.2 2.2 copy-start

commit v3 on v2

--- a/solution.py
+++ b/solution.py
@@ -77,20 +77,25 @@
         def _(i):
             rest[0][i] = acc[i].astype(rest[0].dtype)
     else:
-        sent, own, full = rest[:3]
+        sent, own, full, rounded, sems = rest[:5]
         paired, half = own.shape[0], own.shape[2]
         x = lax.axis_index("col") % 2
         mine = pl.ds(pl.multiple_of(x * half, half), half)
         theirs = pl.ds(pl.multiple_of((1 - x) * half, half), half)
+        full_copy = pltpu.make_async_copy(acc.at[pl.ds(paired, hidden_blocks - paired)], full, sems.at[0])
+        own_copy = pltpu.make_async_copy(acc.at[pl.ds(0, paired), :, mine], own, sems.at[1])
+        full_copy.start()
+        own_copy.start()
 
         @pl.loop(0, paired)
         def _(i):
-            sent[i] = acc[i, :, theirs].astype(sent.dtype)
-            own[i] = acc[i, :, mine]
-
-        @pl.loop(paired, hidden_blocks)
-        def _(i):
-            full[i - paired] = acc[i]
+            rounded[i] = acc[i, :, theirs].astype(rounded.dtype)
+
+        sent_copy = pltpu.make_async_copy(rounded, sent, sems.at[2])
+        sent_copy.start()
+        full_copy.wait()
+        own_copy.wait()
+        sent_copy.wait()
 
 
 def finish_kernel(
@@ -175,6 +180,8 @@
     z, x = col // 2, col % 2
     peer, right, left = z * 2 + (1 - x), col + 2, col - 2
     last = n_z - 1
+    hop = 2
+    lag = hop * last
     half = own.shape[2]
     quarter = full.shape[2] // n_z
     n_a, n_b = own.shape[0], full.shape[0]
@@ -268,7 +275,7 @@
             x_copy(t).wait_recv()
             join(t, own, [from_x])
 
-        r = t - z
+        r = t - hop * z
 
         @pl.when((r >= 0) & (r < n_a) & (z < last))
         def _():
@@ -283,7 +290,7 @@
 
             right_copy(r).start()
 
-        l = t - (last - z)
+        l = t - hop * (last - z)
 
         @pl.when((l >= 0) & (l < n_a) & (z > 0))
         def _():
@@ -298,7 +305,7 @@
 
             left_copy(l).start()
 
-        f = t - n_z
+        f = t - lag
 
         @pl.when((f >= 0) & (f < n_a))
         def _():
@@ -327,7 +334,7 @@
             chain[k, u, rows(d)] = total.astype(chain.dtype)
 
     def chain_step(t):
-        r = t - z
+        r = t - hop * z
 
         @pl.when((r >= 0) & (r < n_b))
         def _():
@@ -345,7 +352,7 @@
 
                     chain_right(r, d).start()
 
-        l = t - (last - z)
+        l = t - hop * (last - z)
 
         @pl.when((l >= 0) & (l < n_b))
         def _():
@@ -363,7 +370,7 @@
 
                     chain_left(l, d).start()
 
-        f = t - n_z
+        f = t - lag
 
         @pl.when((f >= 0) & (f < n_b))
         def _():
@@ -384,7 +391,7 @@
             pair_out[f] = full[f, :, my_quarter].astype(pair_out.dtype)
             pair_copy(f).start()
 
-        g = t - n_z - 2
+        g = t - lag - 3
 
         @pl.when((g >= 0) & (g < n_b))
         def _():
@@ -396,8 +403,8 @@
             pl.when(z > 0)(lambda: gather_left(g, z).start())
 
         for d in range(n_z):
-            right_at = g - (z - d)
-            left_at = g - (d - z)
+            right_at = g - hop * (z - d)
+            left_at = g - hop * (d - z)
 
             @pl.when((d < z) & (right_at >= 0) & (right_at < n_b))
             def _():
@@ -409,13 +416,13 @@
                 gather_left(left_at, d).wait_recv()
                 pl.when(z > 0)(lambda: gather_left(left_at, d).start())
 
-        done = g - last
+        done = g - hop * last
 
         @pl.when((done >= 0) & (done < n_b))
         def _():
             out_copy(done).start()
 
-    @pl.loop(0, max(n_a + n_z, n_b + n_z + 2 + last) + 1)
+    @pl.loop(0, max(n_a + lag, n_b + lag + 3 + hop * last))
     def _(t):
         first = ahead + t + (t + 1) // 2
 
@@ -628,14 +635,16 @@
             jax.ShapeDtypeStruct(half, jnp.float32),
             jax.ShapeDtypeStruct((hidden_blocks - n_a, 3, total, blk), jnp.float32),
         )
+        partial_scratch = [pltpu.VMEM(half, jnp.bfloat16), pltpu.SemaphoreType.DMA((3,))]
     else:
         partial_shape = (jax.ShapeDtypeStruct((hidden_blocks, 3, total, blk), jnp.bfloat16),)
+        partial_scratch = []
     partial = pl.pallas_call(
         partial_kernel,
         out_shape=partial_shape,
         in_specs=[smem] * 5 + [vmem] * 5,
-        out_specs=(vmem,) * len(partial_shape),
-        scratch_shapes=[pltpu.VMEM((hidden_blocks, 3, total, blk), jnp.float32)],
+        out_specs=(pl.BlockSpec(memory_space=pl.ANY) if paired else vmem,) * len(partial_shape),
+        scratch_shapes=partial_scratch + [pltpu.VMEM((hidden_blocks, 3, total, blk), jnp.float32)],
         compiler_params=params,
         name="partial_sums",
     )(pair_slots, down_slots, *exps, tokens_all, grads_all, *values)

time: 303 us -> 304 us (level)
    pallas_call x1, Pallas kernels: 13.8 us -> 20.7 us  [sum_rows(): pl.pallas_call(sum_kernel, out_shape=(result, result), in_specs=[vmem], o...]
    pallas_call x1, Pallas kernels: 21 us -> 16.1 us  [on_device(): pl.pallas_call(partial_kernel, out_shape=partial_shape, in_specs=[smem] *...]
    pallas_call x1, Pallas kernels: 217 us -> 221 us  [exchange(): pl.pallas_call(functools.partial(exchange_kernel, n_z, min(4, n_a)), out_...]
    pallas_call x1, Pallas kernels: 21.8 us -> 17.6 us  [on_device(): pl.pallas_call(finish_kernel, out_shape=(jax.ShapeDtypeStruct((2, total,...]
where the time goes in v3:
time: 304 us; the launch traced here: 300 us
  Pallas kernels  295 us (97%)
  local copies, waits for them, and re-layouts  3.59 us (1%)
    pallas_call x1, Pallas kernels, exchange(): pl.pallas_call(functools.partial(exchange_kernel, n_z, min(4, n_a)), out_...  221 us
    pallas_call x1, Pallas kernels, sum_rows(): pl.pallas_call(sum_kernel, out_shape=(result, result), in_specs=[vmem], o...  20.7 us
    pallas_call x1, Pallas kernels, gather_rows(): pl.pallas_call(gather_kernel, out_shape=(whole, whole), in_specs=[anywher...  20.1 us
    pallas_call x1, Pallas kernels, on_device(): pl.pallas_call(finish_kernel, out_shape=(jax.ShapeDtypeStruct((2, total,...  17.6 us
    pallas_call x1, Pallas kernels, on_device(): pl.pallas_call(partial_kernel, out_shape=partial_shape, in_specs=[smem] *...  16.1 us

profile of v3, /device:TPU:0, one launch (start us, length us, event | category | flops | bytes accessed | tf_op | source)
XLA Modules:
  0.0 299.7 jit_solution(9785541293295554243)
XLA Ops:
  0.6 20.1 %gather_rows.1 = (bf16[256,2048]{1,0:T(8,128)(2,1)}, bf16[256,2048]{1,0:T(8,128)(2,1)}) custom-call(bf16[64,2048]{1,0:T(8,128)(2,1)} %tokens.1, bf16[64,2048]{1,0:T(8,128)(2,1)} %grads.1), custom_call_target="tpu_custom_call" | custom-call | tf_op jit(solution)/shard_map/gather_rows/pallas_call | solution.py:537
  20.8 16.1 %partial_sums.1 = (bf16[34,3,128,128]{3,2,1,0:T(8,128)(2,1)}, f32[34,3,128,128]{3,2,1,0:T(8,128)}, f32[22,3,256,128]{3,2,1,0:T(8,128)}) custom-call(s32[56]{0:T(128)} %bitcast.17, s32[56]{0:T(128)} %bitcast.19, s32[56]{0:T(128)} %bitcast.21, s32[56]{0:T(128)} %bitcast.23, s32[56]{0:T(128)} %bitcast.25, bf16[256,2048]{1,0:T(8,128)(2,1)} %get-tuple-element.16.tokens, ...), custom_call_target="tpu_custom_call" | custom-call | tf_op jit(solution)/shard_map/partial_sums/pallas_call | solution.py:642
  36.9 220.9 %exchange.1.acts = bf16[56,3,256,128]{3,2,1,0:T(8,128)(2,1)} custom-call(bf16[34,3,128,128]{3,2,1,0:T(8,128)(2,1)} %get-tuple-element.18.sent, f32[34,3,128,128]{3,2,1,0:T(8,128)} %get-tuple-element.19.own_in, f32[22,3,256,128]{3,2,1,0:T(8,128)} %get-tuple-element.20.full_in), custom_call_target="tpu_custom_call" | custom-call | tf_op jit(solution)/shard_map/exchange/pallas_call | solution.py:469
  257.8 17.6 %finish.1 = (f32[2,256,2048]{2,1,0:T(8,128)}, bf16[56,128,128]{2,1,0:T(8,128)(2,1)}, bf16[56,128,128]{2,1,0:T(8,128)(2,1)}, bf16[56,128,128]{2,1,0:T(8,128)(2,1)}) custom-call(s32[56]{0:T(128)} %bitcast.18, s32[56]{0:T(128)} %bitcast.20, s32[56]{0:T(128)} %bitcast.22, s32[56]{0:T(128)} %bitcast.24, s32[56]{0:T(128)} %bitcast.26, ...), custom_call_target="tpu_custom_call" | custom-call | tf_op jit(solution)/shard_map/finish/pallas_call | solution.py:653
  275.4 0.0 copy-start
  275.4 2.2 copy-done
  277.6 20.7 %sum_rows.1 = (bf16[64,2048]{1,0:T(8,128)(2,1)S(1)}, bf16[64,2048]{1,0:T(8,128)(2,1)S(1)}) custom-call(f32[2,256,2048]{2,1,0:T(8,128)S(1)} %copy-done), custom_call_target="tpu_custom_call" | custom-call | tf_op jit(solution)/shard_map/sum_rows/pallas_call | solution.py:591
  298.3 0.7 copy.17
  299.0 0.7 copy.18
Async XLA Ops:
  275.4 2.2 copy-start

commit v4 on v3

--- a/solution.py
+++ b/solution.py
@@ -35,10 +35,16 @@
 
 def partial_kernel(
     pair_ids, down_ids, gate_exps, up_exps, down_exps,
-    tokens, grads, gate_values, up_values, down_values,
+    tokens_in, grads_in, gate_in, up_in, down_in,
     *rest,
 ):
-    acc = rest[-1]
+    tokens, grads, gate_values, up_values, down_values, load_sem, acc = rest[-7:]
+    rest = rest[:-6]
+    operands = (tokens_in, grads_in, gate_in, up_in, down_in)
+    places = (tokens, grads, gate_values, up_values, down_values)
+    loads = [pltpu.make_async_copy(src, dst, load_sem.at[n]) for n, (src, dst) in enumerate(zip(operands, places))]
+    for load in loads:
+        load.start()
     slots, blk = gate_values.shape[0], gate_values.shape[1]
     width_blocks = tokens.shape[1] // blk
     hidden_blocks = acc.shape[0]
@@ -47,6 +53,9 @@
     @pl.loop(0, hidden_blocks)
     def _(i):
         acc[i] = jnp.zeros(acc.shape[1:], jnp.float32)
+
+    for load in loads:
+        load.wait()
 
     @pl.loop(0, slots)
     def _(s):
@@ -180,8 +189,8 @@
     z, x = col // 2, col % 2
     peer, right, left = z * 2 + (1 - x), col + 2, col - 2
     last = n_z - 1
-    hop = 2
-    lag = hop * last
+    hop, b_hop = 2, 1
+    lag, b_lag = hop * last, b_hop * last + 1
     half = own.shape[2]
     quarter = full.shape[2] // n_z
     n_a, n_b = own.shape[0], full.shape[0]
@@ -247,7 +256,6 @@
     full_load.start()
     own_load.start()
     full_load.wait()
-    own_load.wait()
 
     def f32(value):
         return value.astype(jnp.float32)
@@ -334,7 +342,7 @@
             chain[k, u, rows(d)] = total.astype(chain.dtype)
 
     def chain_step(t):
-        r = t - hop * z
+        r = t - b_hop * z
 
         @pl.when((r >= 0) & (r < n_b))
         def _():
@@ -352,7 +360,7 @@
 
                     chain_right(r, d).start()
 
-        l = t - hop * (last - z)
+        l = t - b_hop * (last - z)
 
         @pl.when((l >= 0) & (l < n_b))
         def _():
@@ -370,7 +378,7 @@
 
                     chain_left(l, d).start()
 
-        f = t - lag
+        f = t - b_lag
 
         @pl.when((f >= 0) & (f < n_b))
         def _():
@@ -391,7 +399,7 @@
             pair_out[f] = full[f, :, my_quarter].astype(pair_out.dtype)
             pair_copy(f).start()
 
-        g = t - lag - 3
+        g = t - b_lag - 2
 
         @pl.when((g >= 0) & (g < n_b))
         def _():
@@ -403,8 +411,8 @@
             pl.when(z > 0)(lambda: gather_left(g, z).start())
 
         for d in range(n_z):
-            right_at = g - hop * (z - d)
-            left_at = g - hop * (d - z)
+            right_at = g - b_hop * (z - d)
+            left_at = g - b_hop * (d - z)
 
             @pl.when((d < z) & (right_at >= 0) & (right_at < n_b))
             def _():
@@ -416,13 +424,13 @@
                 gather_left(left_at, d).wait_recv()
                 pl.when(z > 0)(lambda: gather_left(left_at, d).start())
 
-        done = g - hop * last
+        done = g - b_hop * last
 
         @pl.when((done >= 0) & (done < n_b))
         def _():
             out_copy(done).start()
 
-    @pl.loop(0, max(n_a + lag, n_b + lag + 3 + hop * last))
+    @pl.loop(0, max(n_a + lag, n_b + b_lag + 2 + b_hop * last))
     def _(t):
         first = ahead + t + (t + 1) // 2
 
@@ -435,6 +443,7 @@
             x_copy(first + 1).start()
 
         chain_step(t)
+        pl.when(t == 0)(lambda: own_load.wait())
         paired_step(t)
 
     @pl.loop(0, n_a)
@@ -545,7 +554,7 @@
     )(tokens, grads)
 
 
-def sum_kernel(parts, output, input_grad, from_near, to_far, from_far, send, recv):
+def sum_kernel(parts, output, input_grad, kept, from_near, to_far, from_far, send, recv, load):
     row, y, core, far, near = row_neighbours()
     share = output.shape[0]
     results = (output, input_grad)
@@ -563,16 +572,22 @@
     def far_copy(u):
         return row_remote(to_far.at[u], from_far.at[u], send.at[2, u], recv.at[2, u], far)
 
+    def load_copy(place, u):
+        return pltpu.make_async_copy(parts.at[u, rows((far, row)[place])], kept.at[place, u], load.at[place, u])
+
     for place in range(2):
         for u in range(2):
             near_copy(place, u).start()
+            load_copy(place, u).start()
     for u in range(2):
+        load_copy(0, u).wait()
         near_copy(0, u).wait_recv()
-        to_far[u] = (parts[u, rows(far)] + from_near[0, u]).astype(to_far.dtype)
+        to_far[u] = (kept[0, u] + from_near[0, u]).astype(to_far.dtype)
         far_copy(u).start()
     for u in range(2):
+        load_copy(1, u).wait()
         near_copy(1, u).wait_recv()
-        from_near[1, u] += parts[u, rows(row)]
+        from_near[1, u] += kept[1, u]
     for u in range(2):
         far_copy(u).wait_recv()
         results[u][...] = (from_near[1, u] + from_far[u].astype(jnp.float32)).astype(jnp.bfloat16)
@@ -591,16 +606,17 @@
     return pl.pallas_call(
         sum_kernel,
         out_shape=(result, result),
-        in_specs=[vmem],
+        in_specs=[pl.BlockSpec(memory_space=pl.ANY)],
         out_specs=(vmem, vmem),
         scratch_shapes=[
             pltpu.VMEM((2, units, share, width), jnp.float32),
+            pltpu.VMEM((2, units, share, width), jnp.float32),
             pltpu.VMEM((units, share, width), jnp.bfloat16),
             pltpu.VMEM((units, share, width), jnp.bfloat16),
-            dma((3, units)), dma((3, units)),
+            dma((3, units)), dma((3, units)), dma((2, units)),
         ],
         compiler_params=pltpu.CompilerParams(
-            collective_id=2, has_side_effects=True, vmem_limit_bytes=32 * 1024 * 1024
+            collective_id=2, has_side_effects=True, vmem_limit_bytes=60 * 1024 * 1024
         ),
         name="sum_rows",
     )(parts)
@@ -628,7 +644,7 @@
     vmem = pl.BlockSpec(memory_space=VMEM)
     params = pltpu.CompilerParams(vmem_limit_bytes=60 * 1024 * 1024)
     if paired:
-        n_a = hidden_blocks * 17 // 28
+        n_a = hidden_blocks * 9 // 14
         half = (n_a, 3, total // 2, blk)
         partial_shape = (
             jax.ShapeDtypeStruct(half, jnp.bfloat16),
@@ -642,9 +658,11 @@
     partial = pl.pallas_call(
         partial_kernel,
         out_shape=partial_shape,
-        in_specs=[smem] * 5 + [vmem] * 5,
+        in_specs=[smem] * 5 + [pl.BlockSpec(memory_space=pl.ANY)] * 5,
         out_specs=(pl.BlockSpec(memory_space=pl.ANY) if paired else vmem,) * len(partial_shape),
-        scratch_shapes=partial_scratch + [pltpu.VMEM((hidden_blocks, 3, total, blk), jnp.float32)],
+        scratch_shapes=partial_scratch
+        + [pltpu.VMEM(each.shape, each.dtype) for each in (tokens_all, grads_all, *values)]
+        + [pltpu.SemaphoreType.DMA((5,)), pltpu.VMEM((hidden_blocks, 3, total, blk), jnp.float32)],
         compiler_params=params,
         name="partial_sums",
     )(pair_slots, down_slots, *exps, tokens_all, grads_all, *values)

time: 304 us -> 292 us (0.961)
  Pallas kernels: 295 us -> 286 us
    pallas_call x1, Pallas kernels: 221 us -> 207 us  [exchange(): pl.pallas_call(functools.partial(exchange_kernel, n_z, min(4, n_a)), out_...]
    pallas_call x1, Pallas kernels: 17.6 us -> 22.7 us  [on_device(): pl.pallas_call(finish_kernel, out_shape=(jax.ShapeDtypeStruct((2, total,...]
    pallas_call x1, Pallas kernels: 20.7 us -> 16.6 us  [sum_rows(): pl.pallas_call(sum_kernel, out_shape=(result, result), in_specs=[pl.Block...]
where the time goes in v4:
time: 292 us; the launch traced here: 290 us
  Pallas kernels  286 us (98%)
  local copies, waits for them, and re-layouts  3.34 us (1%)
    pallas_call x1, Pallas kernels, exchange(): pl.pallas_call(functools.partial(exchange_kernel, n_z, min(4, n_a)), out_...  207 us
    pallas_call x1, Pallas kernels, on_device(): pl.pallas_call(finish_kernel, out_shape=(jax.ShapeDtypeStruct((2, total,...  22.7 us
    pallas_call x1, Pallas kernels, gather_rows(): pl.pallas_call(gather_kernel, out_shape=(whole, whole), in_specs=[anywher...  20.1 us
    pallas_call x1, Pallas kernels, on_device(): pl.pallas_call(partial_kernel, out_shape=partial_shape, in_specs=[smem] *...  19.1 us
    pallas_call x1, Pallas kernels, sum_rows(): pl.pallas_call(sum_kernel, out_shape=(result, result), in_specs=[pl.Block...  16.6 us

profile of v4, /device:TPU:0, one launch (start us, length us, event | category | flops | bytes accessed | tf_op | source)
XLA Modules:
  0.0 289.8 jit_solution(7936531487478078591)
XLA Ops:
  0.6 20.1 %gather_rows.1 = (bf16[256,2048]{1,0:T(8,128)(2,1)}, bf16[256,2048]{1,0:T(8,128)(2,1)}) custom-call(bf16[64,2048]{1,0:T(8,128)(2,1)} %tokens.1, bf16[64,2048]{1,0:T(8,128)(2,1)} %grads.1), custom_call_target="tpu_custom_call" | custom-call | tf_op jit(solution)/shard_map/gather_rows/pallas_call | solution.py:546
  20.8 19.1 %partial_sums.1 = (bf16[36,3,128,128]{3,2,1,0:T(8,128)(2,1)}, f32[36,3,128,128]{3,2,1,0:T(8,128)}, f32[20,3,256,128]{3,2,1,0:T(8,128)}) custom-call(s32[56]{0:T(128)} %bitcast.17, s32[56]{0:T(128)} %bitcast.19, s32[56]{0:T(128)} %bitcast.21, s32[56]{0:T(128)} %bitcast.23, s32[56]{0:T(128)} %bitcast.25, bf16[256,2048]{1,0:T(8,128)(2,1)} %get-tuple-element.16.tokens_in.tokens, ...), custom_call_target="tpu_custom_call" | custom-call | tf_op jit(solution)/shard_map/partial_sums/pallas_call | solution.py:658
  39.9 207.3 %exchange.1.acts = bf16[56,3,256,128]{3,2,1,0:T(8,128)(2,1)} custom-call(bf16[36,3,128,128]{3,2,1,0:T(8,128)(2,1)} %get-tuple-element.18.sent, f32[36,3,128,128]{3,2,1,0:T(8,128)} %get-tuple-element.19.own_in, f32[20,3,256,128]{3,2,1,0:T(8,128)} %get-tuple-element.20.full_in), custom_call_target="tpu_custom_call" | custom-call | tf_op jit(solution)/shard_map/exchange/pallas_call | solution.py:478
  247.2 22.7 %finish.1 = (f32[2,256,2048]{2,1,0:T(8,128)}, bf16[56,128,128]{2,1,0:T(8,128)(2,1)}, bf16[56,128,128]{2,1,0:T(8,128)(2,1)}, bf16[56,128,128]{2,1,0:T(8,128)(2,1)}) custom-call(s32[56]{0:T(128)} %bitcast.18, s32[56]{0:T(128)} %bitcast.20, s32[56]{0:T(128)} %bitcast.22, s32[56]{0:T(128)} %bitcast.24, s32[56]{0:T(128)} %bitcast.26, ...), custom_call_target="tpu_custom_call" | custom-call | tf_op jit(solution)/shard_map/finish/pallas_call | solution.py:671
  269.9 16.6 %sum_rows.1 = (bf16[64,2048]{1,0:T(8,128)(2,1)}, bf16[64,2048]{1,0:T(8,128)(2,1)}) custom-call(f32[2,256,2048]{2,1,0:T(8,128)} %get-tuple-element.21.parts), custom_call_target="tpu_custom_call" | custom-call | tf_op jit(solution)/shard_map/sum_rows/pallas_call | solution.py:606
  286.5 1.7 copy.17
  288.2 1.7 copy.18
